TPU v7x, 32 devices: a whole 2x2x4 slice. The times are simulated.
32 devices in a mesh: ctx: 16 (over z, y, x), tp: 2 (over core).
Axes of the slice: x: 2, y: 2, z: 4, core: 2. Of those that a mesh axis runs over, the one named last changes fastest.
Arguments:
- query_states: bfloat16 [8192, 4096], P('ctx', 'tp'), may hold values from -32 to 32
- rotated_key_states: bfloat16 [8192, 2048], P('ctx', 'tp'), may hold values from -32 to 32
- value_state_rows: bfloat16 [8192, 2048], P('ctx', 'tp'), may hold values from -6 to 6
- doc_ids: int32 [8192], P('ctx'), may hold values from 0 to 7, never falling along the last dimension, each value on 1 to 2048 neighbouring positions
- w_out: bfloat16 [4096, 5376], P('ctx', 'tp'), may hold values from -0.125 to 0.125
Outputs:
- mixed: bfloat16 [8192, 5376], P('ctx', 'tp')
Inputs may be any that keep to these rules, and one draw needn't show every extreme that they name: `doc_ids`: document numbers never fall along the tokens; each document has 1 to 2048 tokens and one has exactly 2048.
All inputs are finite; a program needn't handle non-finite values.
Results may differ from a plain program's by a relative error of at most 0.0054.
Values may be sent and summed in bfloat16 or wider, within the bound.
A program may use at most 128 MiB of HBM per device.

v0:
```python
import jax
import jax.numpy as jnp
from jax import lax
from jax.sharding import PartitionSpec as P

HEAD_SIZE = 128
LOOKBACK_SPAN = 1024


attn_scale = 168.0 ** (-0.5)


def shifted(value, axis, by):
    peers = lax.axis_size(axis)
    pairs = [(i, i + by) for i in range(peers) if 0 <= i + by < peers]
    return lax.ppermute(value, axis, pairs)


def score_block(query_heads, key_block, visible):
    scores = (
        jnp.einsum("qhgd,khd->hgqk", query_heads, key_block, preferred_element_type=jnp.float32)
        * attn_scale
    )
    return jnp.where(visible, scores, -jnp.inf)


def weigh_block(rounded, value_block):
    return jnp.einsum("hgqk,khd->qhgd", rounded, value_block, preferred_element_type=jnp.float32)


def body(query_states, rotated_key_states, value_state_rows, doc_ids, w_out):
    tok_rows = query_states.shape[0]
    reach_count = LOOKBACK_SPAN // tok_rows
    shard_index = lax.axis_index("ctx")
    earlier = [
        shifted((rotated_key_states, value_state_rows, doc_ids), "ctx", distance)
        for distance in range(reach_count, 0, -1)
    ]
    key_all = jnp.concatenate([received[0] for received in earlier] + [rotated_key_states], 0)
    value_all = jnp.concatenate([received[1] for received in earlier] + [value_state_rows], 0)
    doc_all = jnp.concatenate([received[2] for received in earlier] + [doc_ids], 0)
    key_count = key_all.shape[0]
    heads_here = query_states.shape[1] // HEAD_SIZE
    kv_here = rotated_key_states.shape[1] // HEAD_SIZE
    queries_per_group = heads_here // kv_here
    query_heads = query_states.reshape(tok_rows, kv_here, queries_per_group, HEAD_SIZE)
    key_heads = key_all.reshape(key_count, kv_here, HEAD_SIZE)
    value_heads = value_all.reshape(key_count, kv_here, HEAD_SIZE)
    query_pos = shard_index * tok_rows + jnp.arange(tok_rows, dtype=jnp.int32)
    key_pos = (shard_index - reach_count) * tok_rows + jnp.arange(key_count, dtype=jnp.int32)
    distance_grid = query_pos[:, None] - key_pos[None, :]
    visible = (
        (doc_ids[:, None] == doc_all[None, :])
        & (key_pos >= 0)[None, :]
        & (distance_grid >= 0)
        & (distance_grid < LOOKBACK_SPAN)
    )
    scores = score_block(query_heads, key_heads, visible)
    row_max = jnp.max(scores, axis=3, keepdims=True)
    weights = jnp.exp(scores - row_max)
    weight_sum = jnp.sum(weights, axis=3)
    rounded = weights.astype(jnp.bfloat16)
    numer = weigh_block(rounded, value_heads)
    attended = (numer / jnp.transpose(weight_sum, (2, 0, 1))[..., None]).astype(jnp.bfloat16)
    attended = attended.reshape(tok_rows, heads_here * HEAD_SIZE)
    all_heads = lax.all_gather(attended, "tp", axis=1, tiled=True)
    mixed = jnp.dot(
        all_heads,
        lax.all_gather(w_out, "ctx", axis=0, tiled=True),
        preferred_element_type=jnp.float32,
    )
    return mixed.astype(jnp.bfloat16)


def solution(mesh):
    return jax.shard_map(
        body,
        mesh=mesh,
        in_specs=(P("ctx", "tp"), P("ctx", "tp"), P("ctx", "tp"), P("ctx"), P("ctx", "tp")),
        out_specs=P("ctx", "tp"),
        check_vma=False,
    )
```

profile of v0, /device:TPU:0, one launch (start us, length us, event | category | flops | bytes accessed | tf_op | source)
XLA Modules:
  0.0 469.6 jit_solution(1130800589870122227)
XLA Ops:
  6.5 0.0 copy-start.1
  6.5 0.0 all-gather.3.cloned.1.call-start
  6.5 6.0 %collective-permute-start = (bf16[512,1024]{1,0:T(8,128)(2,1)}, bf16[512,1024]{1,0:T(8,128)(2,1)}, u32[]{:S(2)}, u32[]{:S(2)}) collective-permute-start(bf16[512,1024]{1,0:T(8,128)(2,1)} %param.7), channel_id=1, source_target_pairs={{0,4},{2,6},{4,8},{6,10},{8,12},{10,14},{12,16},{14,18},{16,20},{1... | collective-permute-start | bytes 3145736 | tf_op jit(solution)/shard_map/ppermute | solution.py:16
  12.5 4.4 collective-permute-start.1
  16.9 1.5 collective-permute-start.2
  18.4 3.4 collective-permute-start.3
  21.8 2.3 copy.10
  24.1 4.4 collective-permute-start.4
  28.5 29.4 %collective-permute-done.2 = s32[512]{0:T(512)S(1)} collective-permute-done((s32[512]{0:T(512)}, s32[512]{0:T(512)S(1)}, u32[]{:S(2)}, u32[]{:S(2)}) %collective-permute-start.2) | collective-permute-done | bytes 2080 | tf_op jit(solution)/shard_map/ppermute | solution.py:16
  57.9 2.3 collective-permute-start.5
  60.2 3.2 reshape.29
  63.4 0.0 collective-permute-done.3
  63.4 0.0 copy-done.1
  63.5 1.7 fusion.8
  65.2 0.0 collective-permute-done
  65.2 0.0 collective-permute-done.1
  65.2 3.2 pad_maximum_fusion
  68.4 4.6 copy.9
  73.0 28.7 %collective-permute-done.4 = bf16[512,1024]{0,1:T(8,128)(2,1)} collective-permute-done((bf16[512,1024]{0,1:T(8,128)(2,1)}, bf16[512,1024]{0,1:T(8,128)(2,1)}, u32[]{:S(2)}, u32[]{:S(2)}) %collective-permute-start.4) | collective-permute-done | bytes 1048608 | tf_op jit(solution)/shard_map/ppermute | solution.py:16
  101.8 0.0 collective-permute-done.5
  101.8 2.0 pad_maximum_fusion.1
  103.7 19.8 %fusion.2 = (f32[8,2,512]{2,1,0:T(2,128)S(1)}, f32[8,1536,512,2]{2,1,3,0:T(8,128)}) fusion(pred[512,1536]{0,1:T(8,128)(4,1)S(1)} %fusion.8, bf16[1536,8,128,1]{0,2,3,1:T(8,128)(2,1)S(1)} %bitcast.31, bf16[512,8,2,128]{3,2,1,0:T(2,128)(2,1)S(1)} %reshape.29), kind=kOutput, calls=%fused_computation.4 | convolution fusion | flops 3258966016 | bytes 56393728 | tf_op jit(solution)/shard_map/qhgd,khd->hgqk/dot_general | solution.py:21
  123.5 0.0 copy-start
  123.5 21.2 %fusion = f32[8,2,512]{2,1,0:T(2,128)S(1)} fusion(f32[8,1536,512,2]{2,1,3,0:T(8,128)} %get-tuple-element.6, f32[8,2,512]{2,1,0:T(2,128)S(1)} %get-tuple-element.5, pred[512,1536]{0,1:T(8,128)(4,1)S(1)} %fusion.8), kind=kLoop, calls=%fused_computation.2 | loop fusion | flops 50323456 | bytes 51183616 | tf_op jit(solution)/shard_map/reduce_sum | solution.py:61
  144.8 0.0 copy-done
  144.8 22.3 %fusion.6 = bf16[512,8,2,128]{0,3,2,1:T(8,128)(2,1)} fusion(bf16[1536,8,128,1]{0,2,3,1:T(8,128)(2,1)S(1)} %bitcast.32, f32[8,1536,512,2]{2,1,3,0:T(8,128)} %get-tuple-element.6, f32[8,2,512]{2,1,0:T(2,128)S(1)} %get-tuple-element.5, pred[512,1536]{0,1:T(8,128)(4,1)S(1)} %fusion.8, f32[512,8,2]{0,2,1:T(2,128)S(1)} %bitcast.34), kind=kOutput, calls=%fused_computation.11 | convolution fusion | flops 3273654272 | bytes 56426496 | tf_op jit(solution)/shard_map/hgqk,khd->qhgd/dot_general | solution.py:28
  167.1 0.0 all-gather.3.cloned.1.call-update
  167.1 0.2 all-gather.5.cloned.1.call-start
  167.4 0.5 all-gather.5.cloned.1.call-update
  167.9 30.6 %all-gather.3.cloned.1.call-done = bf16[512,4096]{0,1:T(8,128)(2,1)} async-done(((bf16[512,2048]{0,1:T(8,128)(2,1)}), bf16[512,4096]{0,1:T(8,128)(2,1)}) %all-gather.3.cloned.1.call-update) | async-done | bytes 4194320 | tf_op jit(solution)/shard_map/all_gather | solution.py:66
  198.5 245.4 %all-gather.5.cloned.1.call-done = bf16[4096,2688]{1,0:T(8,128)(2,1)} async-done(((bf16[256,2688]{1,0:T(8,128)(2,1)}), bf16[4096,2688]{1,0:T(8,128)(2,1)}) %all-gather.5.cloned.1.call-update) | async-done | bytes 22020112 | tf_op jit(solution)/shard_map/all_gather | solution.py:69
  443.8 19.0 %convolution_convert_fusion = bf16[512,2688]{1,0:T(8,128)(2,1)} fusion(bf16[512,4096]{0,1:T(8,128)(2,1)} %all-gather.3.cloned.1.call-done, bf16[4096,2688]{1,0:T(8,128)(2,1)} %all-gather.5.cloned.1.call-done), kind=kOutput, calls=%fused_computation.9 | convolution fusion | flops 11275665408 | bytes 28966912 | tf_op jit(solution)/shard_map/dot_general | solution.py:67
  (4 shorter events, 0.0 us)
Async XLA Ops:
  6.5 56.9 %copy-start.1 = (s32[512]{0:T(512)S(1)}, s32[512]{0:T(512)}, u32[]{:S(2)}) copy-start(s32[512]{0:T(512)} %param.8) | copy-start | bytes 6148
  6.5 191.9 %all-gather.3.cloned.1.call-start = ((), (), s32[]{:S(2)}) async-start(), calls=%async_computation | async-start | bytes 6291456 | tf_op jit(solution)/shard_map/all_gather | solution.py:66
  6.5 58.6 %collective-permute-start = (bf16[512,1024]{1,0:T(8,128)(2,1)}, bf16[512,1024]{1,0:T(8,128)(2,1)}, u32[]{:S(2)}, u32[]{:S(2)}) collective-permute-start(bf16[512,1024]{1,0:T(8,128)(2,1)} %param.7), channel_id=1, source_target_pairs={{0,4},{2,6},{4,8},{6,10},{8,12},{10,14},{12,16},{14,18},{16,20},{1... | collective-permute-start | bytes 3145736 | tf_op jit(solution)/shard_map/ppermute | solution.py:16
  12.5 52.7 %collective-permute-start.1 = (bf16[512,1024]{1,0:T(8,128)(2,1)}, bf16[512,1024]{1,0:T(8,128)(2,1)}, u32[]{:S(2)}, u32[]{:S(2)}) collective-permute-start(bf16[512,1024]{1,0:T(8,128)(2,1)} %param.7), channel_id=1, source_target_pairs={{0,2},{2,4},{4,6},{6,8},{8,10},{10,12},{12,14},{14,16},{16,18},{18... | collective-permute-start | bytes 3145736 | tf_op jit(solution)/shard_map/ppermute | solution.py:16
  16.9 41.0 %collective-permute-start.2 = (s32[512]{0:T(512)}, s32[512]{0:T(512)S(1)}, u32[]{:S(2)}, u32[]{:S(2)}) collective-permute-start(s32[512]{0:T(512)} %param.8), channel_id=1, source_target_pairs={{0,4},{2,6},{4,8},{6,10},{8,12},{10,14},{12,16},{14,18},{16,20},{1... | collective-permute-start | bytes 6152 | tf_op jit(solution)/shard_map/ppermute | solution.py:16
  18.4 45.1 %collective-permute-start.3 = (s32[512]{0:T(512)}, s32[512]{0:T(512)S(1)}, u32[]{:S(2)}, u32[]{:S(2)}) collective-permute-start(s32[512]{0:T(512)} %param.8), channel_id=1, source_target_pairs={{0,2},{2,4},{4,6},{6,8},{8,10},{10,12},{12,14},{14,16},{16,18},{18... | collective-permute-start | bytes 6152 | tf_op jit(solution)/shard_map/ppermute | solution.py:16
  24.1 77.7 %collective-permute-start.4 = (bf16[512,1024]{0,1:T(8,128)(2,1)}, bf16[512,1024]{0,1:T(8,128)(2,1)}, u32[]{:S(2)}, u32[]{:S(2)}) collective-permute-start(bf16[512,1024]{0,1:T(8,128)(2,1)} %copy.10), channel_id=1, source_target_pairs={{0,4},{2,6},{4,8},{6,10},{8,12},{10,14},{12,16},{14,18},{16,20},{1... | collective-permute-start | bytes 3145736 | tf_op jit(solution)/shard_map/ppermute | solution.py:16
  57.9 43.8 %collective-permute-start.5 = (bf16[512,1024]{0,1:T(8,128)(2,1)}, bf16[512,1024]{0,1:T(8,128)(2,1)}, u32[]{:S(2)}, u32[]{:S(2)}) collective-permute-start(bf16[512,1024]{0,1:T(8,128)(2,1)} %copy.10), channel_id=1, source_target_pairs={{0,2},{2,4},{4,6},{6,8},{8,10},{10,12},{12,14},{14,16},{16,18},{18... | collective-permute-start | bytes 3145736 | tf_op jit(solution)/shard_map/ppermute | solution.py:16
  123.5 21.3 %copy-start = (bf16[1536,1024]{0,1:T(8,128)(2,1)S(1)}, bf16[1536,1024]{0,1:T(8,128)(2,1)}, u32[]{:S(2)}) copy-start(bf16[1536,1024]{0,1:T(8,128)(2,1)} %copy.9) | copy-start | bytes 9437188
  167.1 276.7 %all-gather.5.cloned.1.call-start = ((), (), s32[]{:S(2)}) async-start(), calls=%async_computation.1 | async-start | bytes 23396352 | tf_op jit(solution)/shard_map/all_gather | solution.py:69
Sparse Core Ops, SparseCore 0:
  167.3 31.1 all-gather.2
  201.2 242.5 all-gather.4
where the time goes:
time: 470 us
  waiting for transfers between devices  335 us (71%)
  matrix products  61.1 us (13%)
  other arithmetic  28.1 us (6%)
  starting transfers between devices  22.1 us (5%)
  between operations  13.5 us (3%)
  local copies, waits for them, and re-layouts  10.1 us (2%)
    all_gather x1, waiting for transfers between devices, body(): lax.all_gather(w_out, 'ctx', axis=0, tiled=True)  245 us
    ppermute x6, waiting for transfers between devices, shifted(): return lax.ppermute(value, axis, pairs)  58.2 us
    all_gather x1, waiting for transfers between devices, body(): all_heads = lax.all_gather(attended, 'tp', axis=1, tiled=True)  30.6 us
    dot_general x1, matrix products, weigh_block(): jnp.einsum('hgqk,khd->qhgd', rounded, value_block, preferred_element_type...  22.3 us
    ppermute x6, starting transfers between devices, shifted(): return lax.ppermute(value, axis, pairs)  21.9 us
    reduce_sum x1, other arithmetic, body(): weight_sum = jnp.sum(weights, axis=3)  21.2 us
    dot_general x1, matrix products, score_block(): jnp.einsum('qhgd,khd->hgqk', query_heads, key_block, preferred_element_ty...  19.8 us
    dot_general x1, matrix products, body(): jnp.dot(all_heads, lax.all_gather(w_out, 'ctx', axis=0, tiled=True), pref...  19 us
  transfers between devices with their start and end apart: 8, of which 4 were waited for; matrix products, arithmetic and copies ran while one was open for 3% of the time, Pallas kernels for 0%

commit v1 on v0

v1 whole, which is shorter than its diff:
```python
import functools
import jax
import jax.numpy as jnp
from jax import lax
from jax.experimental import pallas as pl
from jax.experimental.pallas import tpu as pltpu
from jax.sharding import PartitionSpec as P

HEAD_SIZE = 128
LOOKBACK_SPAN = 1024
HIDDEN = -1e30

attn_scale = 168.0 ** (-0.5)
exp2_scale = attn_scale * 1.4426950408889634


def shifted(value, axis, by):
    peers = lax.axis_size(axis)
    pairs = [(i, i + by) for i in range(peers) if 0 <= i + by < peers]
    return lax.ppermute(value, axis, pairs)


def swapped(value, axis):
    return lax.ppermute(value, axis, [(i, i ^ 1) for i in range(lax.axis_size(axis))])


def attend_kernel(blocks, group, tile, *refs):
    q_ref = refs[1]
    k_refs = refs[2 : 2 + blocks]
    v_refs = refs[2 + blocks : 2 + 2 * blocks]
    qdoc_ref, kdoc_ref, o_ref, bias = refs[2 + 2 * blocks :]
    rows = q_ref.shape[0]
    span = LOOKBACK_SPAN + tile

    @pl.when(pl.program_id(0) == 0)
    def _():
        for t in range(rows // tile):
            near = t * tile
            col = lax.broadcasted_iota(jnp.int32, (tile, span), 1)
            row = lax.broadcasted_iota(jnp.int32, (tile, span), 0)
            ahead = row + LOOKBACK_SPAN - col
            same = qdoc_ref[near : near + tile, :] == kdoc_ref[:, near : near + span]
            seen = same & (ahead >= 0) & (ahead < LOOKBACK_SPAN)
            bias[t] = jnp.where(seen, 0.0, HIDDEN)

    def rows_of(block_refs, start, stop):
        pieces = []
        for b, ref in enumerate(block_refs):
            lo, hi = max(start, b * rows), min(stop, (b + 1) * rows)
            if lo < hi:
                pieces.append(ref[lo - b * rows : hi - b * rows, :])
        return jnp.concatenate(pieces, 0) if len(pieces) > 1 else pieces[0]

    for t in range(rows // tile):
        near = t * tile
        keys = rows_of(k_refs, near, near + span)
        values = rows_of(v_refs, near, near + span)
        for h in range(group):
            lanes = slice(h * HEAD_SIZE, (h + 1) * HEAD_SIZE)
            query = q_ref[near : near + tile, lanes]
            s = lax.dot_general(
                query, keys, (((1,), (1,)), ((), ())), preferred_element_type=jnp.float32
            )
            s = s + bias[t]
            top = jnp.max(s, axis=1, keepdims=True)
            w = jnp.exp2((s - top) * exp2_scale)
            total = jnp.sum(w, axis=1, keepdims=True)
            numer = jnp.dot(w.astype(jnp.bfloat16), values, preferred_element_type=jnp.float32)
            o_ref[near : near + tile, lanes] = (numer / total).astype(o_ref.dtype)


def attend(first, stride, query_states, keys, values, query_docs, key_docs):
    rows, width = query_states.shape
    kv_here = keys[0].shape[1] // HEAD_SIZE
    group = width // HEAD_SIZE // kv_here
    blocks = len(keys)
    heads = kv_here // stride
    tile = min(256, rows)
    wide = group * HEAD_SIZE
    span = LOOKBACK_SPAN + tile

    def head(i, first_ref):
        return (0, i * stride + first_ref[0])

    def whole(i, first_ref):
        return (0, 0)

    kv_spec = pl.BlockSpec((rows, HEAD_SIZE), head)
    return pl.pallas_call(
        functools.partial(attend_kernel, blocks, group, tile),
        out_shape=jax.ShapeDtypeStruct((rows, heads * wide), jnp.bfloat16),
        grid_spec=pltpu.PrefetchScalarGridSpec(
            num_scalar_prefetch=1,
            grid=(heads,),
            in_specs=[pl.BlockSpec((rows, wide), head)]
            + [kv_spec] * (2 * blocks)
            + [pl.BlockSpec((rows, 1), whole), pl.BlockSpec((1, blocks * rows), whole)],
            out_specs=pl.BlockSpec((rows, wide), lambda i, first_ref: (0, i)),
            scratch_shapes=[pltpu.VMEM((rows // tile, tile, span), jnp.float32)],
        ),
        compiler_params=pltpu.CompilerParams(vmem_limit_bytes=40 * 1024 * 1024),
        cost_estimate=pl.CostEstimate(
            flops=4 * heads * group * rows * span * HEAD_SIZE,
            bytes_accessed=2 * heads * rows * (2 * wide + 2 * blocks * HEAD_SIZE),
            transcendentals=heads * group * rows * span,
        ),
    )(first, query_states, *keys, *values, query_docs, key_docs)


def body(query_states, rotated_key_states, value_state_rows, doc_ids, w_out):
    tok_rows = query_states.shape[0]
    reach_count = LOOKBACK_SPAN // tok_rows
    shard_index = lax.axis_index("ctx")
    ctx, tp = lax.axis_size("ctx"), lax.axis_size("tp")
    kv_here = rotated_key_states.shape[1] // HEAD_SIZE
    columns = w_out.shape[1]
    half = -(-columns // 256) * 128
    paired = (
        ctx % 2 == 0
        and tp == 2
        and kv_here % 2 == 0
        and w_out.shape[0] * kv_here == query_states.shape[1]
        and columns % 128 == 0
    )
    parity = shard_index % 2

    docs, keys, values = [doc_ids], [rotated_key_states], [value_state_rows]
    for distance in range(1, reach_count + 1):
        got = shifted(doc_ids, "ctx", distance)
        docs.insert(0, jnp.where(shard_index >= distance, got, -1))
        keys.insert(0, shifted(rotated_key_states, "ctx", distance))
        values.insert(0, shifted(value_state_rows, "ctx", distance))
    query_docs = doc_ids[:, None]
    key_docs = jnp.concatenate(docs)[None, :]

    if not paired:
        all_w = lax.all_gather(w_out, "ctx", axis=0, tiled=True)
        first = jnp.zeros((1,), jnp.int32)
        attended = attend(first, 1, query_states, keys, values, query_docs, key_docs)
        all_heads = lax.all_gather(attended, "tp", axis=1, tiled=True)
        mixed = jnp.dot(all_heads, all_w, preferred_element_type=jnp.float32)
        return mixed.astype(jnp.bfloat16)

    shift = columns - half
    groups = [list(range(p, ctx, 2)) for p in range(2)]
    w_mine = lax.dynamic_slice_in_dim(w_out, parity * shift, half, 1)
    w_theirs = lax.dynamic_slice_in_dim(w_out, (1 - parity) * shift, half, 1)
    near_w = lax.all_gather(w_mine, "ctx", axis=0, tiled=True, axis_index_groups=groups)
    w_came = swapped(w_theirs, "ctx")
    far_w = lax.all_gather(w_came, "ctx", axis=0, tiled=True, axis_index_groups=groups)

    core = lax.axis_index("tp")

    def both_cores(part):
        other = swapped(part, "tp")
        low = jnp.where(core == 0, part, other)
        high = jnp.where(core == 0, other, part)
        return jnp.concatenate([low, high], 1)

    def heads_of(which):
        return attend(
            which.reshape(1).astype(jnp.int32), 2, query_states, keys, values, query_docs, key_docs
        )

    mine_near = heads_of(parity)
    theirs_far = swapped(mine_near, "ctx")
    mine_far = heads_of(1 - parity)
    theirs_near = swapped(mine_far, "ctx")

    def project(near, far):
        total = jnp.dot(both_cores(near), near_w, preferred_element_type=jnp.float32)
        total = total + jnp.dot(both_cores(far), far_w, preferred_element_type=jnp.float32)
        return total.astype(jnp.bfloat16)

    came = swapped(project(theirs_near, theirs_far), "ctx")
    made = project(mine_near, mine_far)
    left = jnp.where(parity == 0, made, came)
    right = jnp.where(parity == 0, came, made)
    return jnp.concatenate([left, right[:, 2 * half - columns :]], 1)


def solution(mesh):
    return jax.shard_map(
        body,
        mesh=mesh,
        in_specs=(P("ctx", "tp"), P("ctx", "tp"), P("ctx", "tp"), P("ctx"), P("ctx", "tp")),
        out_specs=P("ctx", "tp"),
        check_vma=False,
    )
```

time: 470 us -> 350 us (0.74)
  waiting for transfers between devices: 335 us -> 238 us
  matrix products: 61.1 us -> 24.1 us
  Pallas kernels: 0 us -> 24.7 us
  other arithmetic: 28.1 us -> 11.1 us
  starting transfers between devices: 22.1 us -> 28.7 us
    all_gather x2, waiting for transfers between devices: 276 us -> 68.7 us  [the longest x1 68.7 us: body(): lax.all_gather(w_mine, 'ctx', axis=0, tiled=True, axis_index_groups=groups)]
    ppermute x0 -> x8, waiting for transfers between devices: none -> 68.5 us  [swapped(): lax.ppermute(value, axis, [(i, i ^ 1) for i in range(lax.axis_size(axis))])]
    ppermute x6, waiting for transfers between devices: 58.2 us -> 100 us  [shifted(): return lax.ppermute(value, axis, pairs)]
    dot_general x3 -> x4, matrix products: 61.1 us -> 24.1 us  [the longest x2 12.4 us: project(): jnp.dot(both_cores(near), near_w, preferred_element_type=jnp.float32)]
    pallas_call x0 -> x2, Pallas kernels: none -> 24.7 us  [attend(): pl.pallas_call(functools.partial(attend_kernel, blocks, group, tile), out...]
    reduce_sum x1 -> x0, other arithmetic: 21.2 us -> none  [body(): weight_sum = jnp.sum(weights, axis=3)]
    ppermute x0 -> x8, starting transfers between devices: none -> 9.99 us  [swapped(): lax.ppermute(value, axis, [(i, i ^ 1) for i in range(lax.axis_size(axis))])]
    select_n x0 -> x7, other arithmetic: none -> 9.39 us  [the longest x4 7.86 us: both_cores(): low = jnp.where(core == 0, part, other)]
  transfers between devices with their start and end apart: 8 -> 16, of which waited for: 4 -> 8; matrix products, arithmetic and copies ran while one was open for 3% -> 8% of each run, Pallas kernels for 0% -> 7%
where the time goes in v1:
time: 350 us; the launch traced here: 349 us
  waiting for transfers between devices  238 us (68%)
  starting transfers between devices  28.7 us (8%)
  Pallas kernels  24.7 us (7%)
  matrix products  24.1 us (7%)
  between operations  13.6 us (4%)
  other arithmetic  11.1 us (3%)
  local copies, waits for them, and re-layouts  8.67 us (2%)
    ppermute x6, waiting for transfers between devices, shifted(): return lax.ppermute(value, axis, pairs)  100 us
    all_gather x1, waiting for transfers between devices, body(): lax.all_gather(w_mine, 'ctx', axis=0, tiled=True, axis_index_groups=groups)  68.7 us
    ppermute x8, waiting for transfers between devices, swapped(): lax.ppermute(value, axis, [(i, i ^ 1) for i in range(lax.axis_size(axis))])  68.5 us
    pallas_call x2, Pallas kernels, attend(): pl.pallas_call(functools.partial(attend_kernel, blocks, group, tile), out...  24.7 us
    ppermute x6, starting transfers between devices, shifted(): return lax.ppermute(value, axis, pairs)  18.6 us
    dot_general x2, matrix products, project(): jnp.dot(both_cores(near), near_w, preferred_element_type=jnp.float32)  12.4 us
    dot_general x2, matrix products, project(): jnp.dot(both_cores(far), far_w, preferred_element_type=jnp.float32)  11.7 us
    ppermute x8, starting transfers between devices, swapped(): lax.ppermute(value, axis, [(i, i ^ 1) for i in range(lax.axis_size(axis))])  9.99 us
  transfers between devices with their start and end apart: 16, of which 8 were waited for; matrix products, arithmetic and copies ran while one was open for 8% of the time, Pallas kernels for 7%

profile of v1, /device:TPU:0, one launch (start us, length us, event | category | flops | bytes accessed | tf_op | source)
XLA Modules:
  0.0 349.1 jit_solution(8684041791146382818)
XLA Ops:
  6.5 0.0 copy-start.2
  6.5 0.0 copy-start.3
  6.5 0.0 all-gather.5.cloned.1.call-start
  6.5 2.5 constant_dynamic-slice_fusion.1
  9.0 2.9 collective-permute-start.8
  11.9 16.1 %collective-permute-done.8 = bf16[256,1408]{1,0:T(8,128)(2,1)S(1)} collective-permute-done((bf16[256,1408]{1,0:T(8,128)(2,1)S(1)}, bf16[256,1408]{1,0:T(8,128)(2,1)S(1)}, u32[]{:S(2)}, u32[]{:S(2)}) %collective-permute-start.8) | collective-permute-done | bytes 720928 | tf_op jit(solution)/shard_map/ppermute | solution.py:24
  28.1 0.9 copy-done.7
  29.0 0.0 all-gather.5.cloned.1.call-update
  29.0 0.0 all-gather.3.cloned.1.call-start
  29.1 0.7 all-gather.3.cloned.1.call-update
  29.8 0.0 copy-done.2
  29.8 3.7 %collective-permute-start = (bf16[512,1024]{1,0:T(8,128)(2,1)S(1)}, bf16[512,1024]{1,0:T(8,128)(2,1)S(1)}, u32[]{:S(2)}, u32[]{:S(2)}) collective-permute-start(bf16[512,1024]{1,0:T(8,128)(2,1)S(1)} %copy-done.2), channel_id=1, source_target_pairs={{0,4},{2,6},{4,8},{6,10},{8,12},{10,14},{12,16},{14,18},{16,20},{1... | collective-permute-start | bytes 3145736 | tf_op jit(solution)/shard_map/ppermute | solution.py:20
  33.5 4.4 %collective-permute-start.1 = (bf16[512,1024]{1,0:T(8,128)(2,1)S(1)}, bf16[512,1024]{1,0:T(8,128)(2,1)}, u32[]{:S(2)}, u32[]{:S(2)}) collective-permute-start(bf16[512,1024]{1,0:T(8,128)(2,1)S(1)} %copy-done.2), channel_id=1, source_target_pairs={{0,2},{2,4},{4,6},{6,8},{8,10},{10,12},{12,14},{14,16},{16,18},{18... | collective-permute-start | bytes 3145736 | tf_op jit(solution)/shard_map/ppermute | solution.py:20
  37.9 0.0 copy-done.3
  37.9 3.4 collective-permute-start.2
  41.3 4.4 %collective-permute-start.3 = (bf16[512,1024]{1,0:T(8,128)(2,1)S(1)}, bf16[512,1024]{1,0:T(8,128)(2,1)}, u32[]{:S(2)}, u32[]{:S(2)}) collective-permute-start(bf16[512,1024]{1,0:T(8,128)(2,1)S(1)} %copy-done.3), channel_id=1, source_target_pairs={{0,2},{2,4},{4,6},{6,8},{8,10},{10,12},{12,14},{14,16},{16,18},{18... | collective-permute-start | bytes 3145736 | tf_op jit(solution)/shard_map/ppermute | solution.py:20
  45.7 0.0 copy-done.8
  45.7 1.4 collective-permute-start.4
  47.2 0.1 copy.6.refs_8_
  47.3 99.0 %collective-permute-done.4 = s32[512]{0:T(512)S(1)} collective-permute-done((s32[512]{0:T(512)S(1)}, s32[512]{0:T(512)S(1)}, u32[]{:S(2)}, u32[]{:S(2)}) %collective-permute-start.4) | collective-permute-done | bytes 2080 | tf_op jit(solution)/shard_map/ppermute | solution.py:20
  146.4 1.3 collective-permute-start.5
  147.7 1.3 collective-permute-done.5
  149.0 0.0 collective-permute-done.refs_2_
  149.0 0.0 copy-start.5
  149.0 1.0 copy-done.5
  150.0 0.0 collective-permute-done.1.refs_3_
  150.0 0.0 collective-permute-done.2.refs_5_
  150.0 0.0 collective-permute-done.3.refs_6_
  150.0 0.0 copy-start
  150.0 1.6 copy-done
  151.6 1.2 copy-done.6
  152.9 12.3 %shard_map.56 = bf16[512,1024]{1,0:T(8,128)(2,1)S(1)} custom-call(s32[1]{0:T(128)} %bitcast.2.refs_0_, bf16[512,2048]{1,0:T(8,128)(2,1)S(1)} %copy-done, bf16[512,1024]{1,0:T(8,128)(2,1)S(1)} %copy-done.6, bf16[512,1024]{1,0:T(8,128)(2,1)} %collective-permute-done.1.refs_3_, bf16[512,1024]{1,0:T(8,128)(2,1)S(1)} %copy-done.2, ...), custom_call_target="tpu_custom_call" | custom-call | flops 2684354560 | bytes 5242880 | tf_op jit(solution)/shard_map/pallas_call | solution.py:89
  165.2 4.9 %collective-permute-start.9 = (bf16[512,1024]{1,0:T(8,128)(2,1)S(1)}, bf16[512,1024]{1,0:T(8,128)(2,1)}, u32[]{:S(2)}, u32[]{:S(2)}) collective-permute-start(bf16[512,1024]{1,0:T(8,128)(2,1)S(1)} %shard_map.56), channel_id=1, source_target_pairs={{0,2},{2,0},{4,6},{6,4},{8,10},{10,8},{12,14},{14,12},{16,18},{18,... | collective-permute-start | bytes 3145736 | tf_op jit(solution)/shard_map/ppermute | solution.py:24
  170.1 0.0 copy-done.1
  170.1 0.0 copy-done.4
  170.1 12.4 %shard_map.55 = bf16[512,1024]{1,0:T(8,128)(2,1)S(1)} custom-call(s32[1]{0:T(128)} %bitcast.refs_0_, bf16[512,2048]{1,0:T(8,128)(2,1)S(1)} %copy-done.1, bf16[512,1024]{1,0:T(8,128)(2,1)S(1)} %copy-done.6, bf16[512,1024]{1,0:T(8,128)(2,1)} %collective-permute-done.1.refs_3_, bf16[512,1024]{1,0:T(8,128)(2,1)S(1)} %copy-done.2, ...), custom_call_target="tpu_custom_call" | custom-call | flops 2684354560 | bytes 5242880 | tf_op jit(solution)/shard_map/pallas_call | solution.py:89
  182.5 0.1 collective-permute-start.11
  182.7 11.6 %collective-permute-done.9 = bf16[512,1024]{1,0:T(8,128)(2,1)} collective-permute-done((bf16[512,1024]{1,0:T(8,128)(2,1)S(1)}, bf16[512,1024]{1,0:T(8,128)(2,1)}, u32[]{:S(2)}, u32[]{:S(2)}) %collective-permute-start.9) | collective-permute-done | bytes 1048608 | tf_op jit(solution)/shard_map/ppermute | solution.py:24
  194.3 0.0 collective-permute-start.10
  194.3 14.8 %collective-permute-done.11 = bf16[512,1024]{1,0:T(8,128)(2,1)} collective-permute-done((bf16[512,1024]{1,0:T(8,128)(2,1)S(1)}, bf16[512,1024]{1,0:T(8,128)(2,1)}, u32[]{:S(2)}, u32[]{:S(2)}) %collective-permute-start.11) | collective-permute-done | bytes 1048608 | tf_op jit(solution)/shard_map/ppermute | solution.py:24
  209.2 0.0 collective-permute-start.12
  209.2 0.5 collective-permute-start.7
  209.7 0.0 collective-permute-start.6
  209.7 0.0 collective-permute-done.10
  209.7 3.2 broadcast_select_fusion.4
  212.9 0.8 collective-permute-done.12
  213.6 3.0 broadcast_select_fusion.2
  216.7 8.3 %fusion.12 = f32[512,1408]{1,0:T(8,128)} fusion(bf16[2048,1408]{1,0:T(8,128)(2,1)} %all-gather.5.cloned.1.call-done, bf16[512,1024]{1,0:T(8,128)(2,1)} %get-tuple-element.8, bf16[512,1024]{1,0:T(8,128)(2,1)} %get-tuple-element.7), kind=kOutput, calls=%fused_computation.15 | convolution fusion | flops 2956984320 | bytes 10747904 | tf_op jit(solution)/shard_map/dot_general | solution.py:172
  225.0 68.7 %all-gather.3.cloned.1.call-done = bf16[2048,1408]{1,0:T(8,128)(2,1)} async-done(((bf16[256,1408]{1,0:T(8,128)(2,1)}), bf16[2048,1408]{1,0:T(8,128)(2,1)}) %all-gather.3.cloned.1.call-update) | async-done | bytes 5767184 | tf_op jit(solution)/shard_map/all_gather | solution.py:148
  293.6 8.6 %fusion.1 = bf16[512,1408]{1,0:T(8,128)(2,1)} fusion(f32[512,1408]{1,0:T(8,128)} %fusion.12, bf16[2048,1408]{1,0:T(8,128)(2,1)} %all-gather.3.cloned.1.call-done, bf16[512,1024]{1,0:T(8,128)(2,1)} %get-tuple-element.6, bf16[512,1024]{1,0:T(8,128)(2,1)} %get-tuple-element.5), kind=kOutput, calls=%fused_computation.3 | convolution fusion | flops 2958426112 | bytes 12189696 | tf_op jit(solution)/shard_map/dot_general | solution.py:171
  302.3 1.5 collective-permute-start.13
  303.7 0.0 collective-permute-done.7
  303.7 1.5 broadcast_select_fusion.6
  305.3 0.0 collective-permute-done.6
  305.3 0.0 slice-start
  305.3 0.1 broadcast_select_fusion.8
  305.4 1.3 copy-done.9
  306.7 3.4 fusion.5
  310.1 25.1 %collective-permute-done.13 = bf16[512,1408]{1,0:T(8,128)(2,1)} collective-permute-done((bf16[512,1408]{1,0:T(8,128)(2,1)}, bf16[512,1408]{1,0:T(8,128)(2,1)}, u32[]{:S(2)}, u32[]{:S(2)}) %collective-permute-start.13) | collective-permute-done | bytes 1441824 | tf_op jit(solution)/shard_map/ppermute | solution.py:24
  335.2 0.0 slice-done
  335.2 0.0 slice-done.1
  335.2 3.8 %broadcast_select_fusion = (bf16[512,1408]{1,0:T(8,128)(2,1)S(1)}, bf16[512,1408]{1,0:T(8,128)(2,1)S(1)}) fusion(bf16[512,1408]{1,0:T(8,128)(2,1)} %collective-permute-done.13, pred[]{:T(512)S(6)} %eq.6, f32[512,1408]{1,0:T(8,128)S(1)} %fusion.5, bf16[2048,1408]{1,0:T(8,128)(2,1)S(1)} %bitcast.9, bf16[512,1024]{1,0:T(8,128)(2,1)S(1)} %get-tuple-element.10, ...), kind=kOutput, calls=%fused_computation.19 | convolution fusion | flops 2959147008 | bytes 15073281 | tf_op jit(solution)/shard_map/dot_general | solution.py:171
  339.0 1.5 slice_select_fusion
  340.5 1.7 pad_maximum_fusion
  (13 shorter events, 0.0 us)
Async XLA Ops:
  6.5 23.2 %copy-start.2 = (bf16[512,1024]{1,0:T(8,128)(2,1)S(1)}, bf16[512,1024]{1,0:T(8,128)(2,1)}, u32[]{:S(2)}) copy-start(bf16[512,1024]{1,0:T(8,128)(2,1)} %refs_4_.3) | copy-start | bytes 3145732
  6.5 31.4 %copy-start.3 = (bf16[512,1024]{1,0:T(8,128)(2,1)S(1)}, bf16[512,1024]{1,0:T(8,128)(2,1)}, u32[]{:S(2)}) copy-start(bf16[512,1024]{1,0:T(8,128)(2,1)} %refs_7_.3) | copy-start | bytes 3145732
  6.5 39.2 %copy-start.8 = (s32[512]{0:T(512)S(1)}, s32[512]{0:T(512)}, u32[]{:S(2)}) copy-start(s32[512]{0:T(512)} %param.8) | copy-start | bytes 6148
  6.5 210.1 %all-gather.5.cloned.1.call-start = ((), (), s32[]{:S(2)}) async-start(), calls=%async_computation.1 | async-start | bytes 6488064 | tf_op jit(solution)/shard_map/all_gather | solution.py:150
  9.0 19.1 %collective-permute-start.8 = (bf16[256,1408]{1,0:T(8,128)(2,1)S(1)}, bf16[256,1408]{1,0:T(8,128)(2,1)S(1)}, u32[]{:S(2)}, u32[]{:S(2)}) collective-permute-start(bf16[256,1408]{1,0:T(8,128)(2,1)S(1)} %get-tuple-element.14), channel_id=1, source_target_pairs={{0,2},{2,0},{4,6},{6,4},{8,10},{10,8},{12,14},{14,12},{16,18},{18,... | collective-permute-start | bytes 2162696 | tf_op jit(solution)/shard_map/ppermute | solution.py:24
  28.1 0.9 copy-start.7
  29.0 264.6 %all-gather.3.cloned.1.call-start = ((), (), s32[]{:S(2)}) async-start(), calls=%async_computation | async-start | bytes 6488064 | tf_op jit(solution)/shard_map/all_gather | solution.py:148
  29.8 119.2 %collective-permute-start = (bf16[512,1024]{1,0:T(8,128)(2,1)S(1)}, bf16[512,1024]{1,0:T(8,128)(2,1)S(1)}, u32[]{:S(2)}, u32[]{:S(2)}) collective-permute-start(bf16[512,1024]{1,0:T(8,128)(2,1)S(1)} %copy-done.2), channel_id=1, source_target_pairs={{0,4},{2,6},{4,8},{6,10},{8,12},{10,14},{12,16},{14,18},{16,20},{1... | collective-permute-start | bytes 3145736 | tf_op jit(solution)/shard_map/ppermute | solution.py:20
  33.5 116.4 %collective-permute-start.1 = (bf16[512,1024]{1,0:T(8,128)(2,1)S(1)}, bf16[512,1024]{1,0:T(8,128)(2,1)}, u32[]{:S(2)}, u32[]{:S(2)}) collective-permute-start(bf16[512,1024]{1,0:T(8,128)(2,1)S(1)} %copy-done.2), channel_id=1, source_target_pairs={{0,2},{2,4},{4,6},{6,8},{8,10},{10,12},{12,14},{14,16},{16,18},{18... | collective-permute-start | bytes 3145736 | tf_op jit(solution)/shard_map/ppermute | solution.py:20
  37.9 112.1 %collective-permute-start.2 = (bf16[512,1024]{1,0:T(8,128)(2,1)S(1)}, bf16[512,1024]{1,0:T(8,128)(2,1)}, u32[]{:S(2)}, u32[]{:S(2)}) collective-permute-start(bf16[512,1024]{1,0:T(8,128)(2,1)S(1)} %copy-done.3), channel_id=1, source_target_pairs={{0,4},{2,6},{4,8},{6,10},{8,12},{10,14},{12,16},{14,18},{16,20},{1... | collective-permute-start | bytes 3145736 | tf_op jit(solution)/shard_map/ppermute | solution.py:20
  41.3 108.7 %collective-permute-start.3 = (bf16[512,1024]{1,0:T(8,128)(2,1)S(1)}, bf16[512,1024]{1,0:T(8,128)(2,1)}, u32[]{:S(2)}, u32[]{:S(2)}) collective-permute-start(bf16[512,1024]{1,0:T(8,128)(2,1)S(1)} %copy-done.3), channel_id=1, source_target_pairs={{0,2},{2,4},{4,6},{6,8},{8,10},{10,12},{12,14},{14,16},{16,18},{18... | collective-permute-start | bytes 3145736 | tf_op jit(solution)/shard_map/ppermute | solution.py:20
  45.7 100.6 %collective-permute-start.4 = (s32[512]{0:T(512)S(1)}, s32[512]{0:T(512)S(1)}, u32[]{:S(2)}, u32[]{:S(2)}) collective-permute-start(s32[512]{0:T(512)S(1)} %copy-done.8), channel_id=1, source_target_pairs={{0,4},{2,6},{4,8},{6,10},{8,12},{10,14},{12,16},{14,18},{16,20},{1... | collective-permute-start | bytes 6152 | tf_op jit(solution)/shard_map/ppermute | solution.py:20
  146.4 2.6 collective-permute-start.5
  149.0 1.0 copy-start.5
  150.0 1.7 copy-start
  151.6 1.2 copy-start.6
  152.9 17.3 %copy-start.1 = (bf16[512,2048]{1,0:T(8,128)(2,1)S(1)}, bf16[512,2048]{1,0:T(8,128)(2,1)}, u32[]{:S(2)}) copy-start(bf16[512,2048]{1,0:T(8,128)(2,1)} %refs_1_.3) | copy-start | bytes 6291460
  152.9 17.3 %copy-start.4 = (bf16[512,1024]{1,0:T(8,128)(2,1)S(1)}, bf16[512,1024]{1,0:T(8,128)(2,1)}, u32[]{:S(2)}) copy-start(bf16[512,1024]{1,0:T(8,128)(2,1)} %refs_7_.3) | copy-start | bytes 3145732
  165.2 29.1 %collective-permute-start.9 = (bf16[512,1024]{1,0:T(8,128)(2,1)S(1)}, bf16[512,1024]{1,0:T(8,128)(2,1)}, u32[]{:S(2)}, u32[]{:S(2)}) collective-permute-start(bf16[512,1024]{1,0:T(8,128)(2,1)S(1)} %shard_map.56), channel_id=1, source_target_pairs={{0,2},{2,0},{4,6},{6,4},{8,10},{10,8},{12,14},{14,12},{16,18},{18,... | collective-permute-start | bytes 3145736 | tf_op jit(solution)/shard_map/ppermute | solution.py:24
  182.5 26.6 %collective-permute-start.11 = (bf16[512,1024]{1,0:T(8,128)(2,1)S(1)}, bf16[512,1024]{1,0:T(8,128)(2,1)}, u32[]{:S(2)}, u32[]{:S(2)}) collective-permute-start(bf16[512,1024]{1,0:T(8,128)(2,1)S(1)} %shard_map.55), channel_id=1, source_target_pairs={{0,2},{2,0},{4,6},{6,4},{8,10},{10,8},{12,14},{14,12},{16,18},{18,... | collective-permute-start | bytes 3145736 | tf_op jit(solution)/shard_map/ppermute | solution.py:24
  194.3 15.4 %collective-permute-start.10 = (bf16[512,1024]{1,0:T(8,128)(2,1)}, bf16[512,1024]{1,0:T(8,128)(2,1)}, u32[]{:S(2)}, u32[]{:S(2)}) collective-permute-start(bf16[512,1024]{1,0:T(8,128)(2,1)} %collective-permute-done.9), channel_id=1, source_target_pairs={{0,1},{1,0},{2,3},{3,2},{4,5},{5,4},{6,7},{7,6},{8,9},{9,8},{10,11... | collective-permute-start | bytes 3145736 | tf_op jit(solution)/shard_map/ppermute | solution.py:24
  209.2 4.5 %collective-permute-start.12 = (bf16[512,1024]{1,0:T(8,128)(2,1)}, bf16[512,1024]{1,0:T(8,128)(2,1)}, u32[]{:S(2)}, u32[]{:S(2)}) collective-permute-start(bf16[512,1024]{1,0:T(8,128)(2,1)} %collective-permute-done.11), channel_id=1, source_target_pairs={{0,1},{1,0},{2,3},{3,2},{4,5},{5,4},{6,7},{7,6},{8,9},{9,8},{10,11... | collective-permute-start | bytes 3145736 | tf_op jit(solution)/shard_map/ppermute | solution.py:24
  209.2 94.6 %collective-permute-start.7 = (bf16[512,1024]{1,0:T(8,128)(2,1)S(1)}, bf16[512,1024]{1,0:T(8,128)(2,1)}, u32[]{:S(2)}, u32[]{:S(2)}) collective-permute-start(bf16[512,1024]{1,0:T(8,128)(2,1)S(1)} %shard_map.56), channel_id=1, source_target_pairs={{0,1},{1,0},{2,3},{3,2},{4,5},{5,4},{6,7},{7,6},{8,9},{9,8},{10,11... | collective-permute-start | bytes 3145736 | tf_op jit(solution)/shard_map/ppermute | solution.py:24
  209.7 95.6 %collective-permute-start.6 = (bf16[512,1024]{1,0:T(8,128)(2,1)S(1)}, bf16[512,1024]{1,0:T(8,128)(2,1)S(1)}, u32[]{:S(2)}, u32[]{:S(2)}) collective-permute-start(bf16[512,1024]{1,0:T(8,128)(2,1)S(1)} %shard_map.55), channel_id=1, source_target_pairs={{0,1},{1,0},{2,3},{3,2},{4,5},{5,4},{6,7},{7,6},{8,9},{9,8},{10,11... | collective-permute-start | bytes 3145736 | tf_op jit(solution)/shard_map/ppermute | solution.py:24
  302.3 33.0 %collective-permute-start.13 = (bf16[512,1408]{1,0:T(8,128)(2,1)}, bf16[512,1408]{1,0:T(8,128)(2,1)}, u32[]{:S(2)}, u32[]{:S(2)}) collective-permute-start(bf16[512,1408]{1,0:T(8,128)(2,1)} %fusion.1), channel_id=1, source_target_pairs={{0,2},{2,0},{4,6},{6,4},{8,10},{10,8},{12,14},{14,12},{16,18},{18,... | collective-permute-start | bytes 4325384 | tf_op jit(solution)/shard_map/ppermute | solution.py:24
  303.7 3.0 copy-start.9
  305.3 30.0 %slice-start = ((s8[5767168]{0:T(1024)(128)(4,1)}), s8[4194304]{0:T(1024)(128)(4,1)S(1)}, s32[]{:S(2)}) async-start(s8[5767168]{0:T(1024)(128)(4,1)} %bitcast.8), calls=%async_computation.2 | async-start | bytes 8388608
  306.7 28.5 %slice-start.1 = ((s8[5767168]{0:T(1024)(128)(4,1)}), s8[1572864]{0:T(1024)(128)(4,1)S(1)}, s32[]{:S(2)}) async-start(s8[5767168]{0:T(1024)(128)(4,1)} %bitcast.8), calls=%async_computation.3 | async-start | bytes 3145728
Sparse Core Ops, SparseCore 0:
  29.1 140.2 all-gather.4
  171.6 121.9 all-gather.2

commit v2 on v1

--- a/solution.py
+++ b/solution.py
@@ -22,6 +22,30 @@
 
 def swapped(value, axis):
     return lax.ppermute(value, axis, [(i, i ^ 1) for i in range(lax.axis_size(axis))])
+
+
+def ring_gather(forward, backward):
+    ctx = lax.axis_size("ctx")
+    n = ctx // 2
+    ring = list(range(0, n, 2)) + list(range(n - 1, 0, -2))
+    place = lax.axis_index("ctx") // 2
+    at = jnp.where(place % 2 == 0, place // 2, n - 1 - place // 2)
+    rows, width = forward.shape
+    held = [forward, backward]
+    full = [jnp.zeros((n * rows, width), forward.dtype) for _ in held]
+    for step in range(n):
+        for way, sign in enumerate((1, -1)):
+            if step:
+                hops = [
+                    (2 * ring[k] + p, 2 * ring[(k + sign) % n] + p)
+                    for k in range(n)
+                    for p in range(2)
+                ]
+                held[way] = lax.ppermute(held[way], "ctx", hops)
+            k = (at - sign * step + n) % n
+            origin = jnp.where(k < n // 2, 2 * k, 2 * (n - 1 - k) + 1)
+            full[way] = lax.dynamic_update_slice_in_dim(full[way], held[way], origin * rows, 0)
+    return full
 
 
 def attend_kernel(blocks, group, tile, *refs):
@@ -116,7 +140,7 @@
     columns = w_out.shape[1]
     half = -(-columns // 256) * 128
     paired = (
-        ctx % 2 == 0
+        ctx % 4 == 0
         and tp == 2
         and kv_here % 2 == 0
         and w_out.shape[0] * kv_here == query_states.shape[1]
@@ -142,12 +166,9 @@
         return mixed.astype(jnp.bfloat16)
 
     shift = columns - half
-    groups = [list(range(p, ctx, 2)) for p in range(2)]
     w_mine = lax.dynamic_slice_in_dim(w_out, parity * shift, half, 1)
     w_theirs = lax.dynamic_slice_in_dim(w_out, (1 - parity) * shift, half, 1)
-    near_w = lax.all_gather(w_mine, "ctx", axis=0, tiled=True, axis_index_groups=groups)
-    w_came = swapped(w_theirs, "ctx")
-    far_w = lax.all_gather(w_came, "ctx", axis=0, tiled=True, axis_index_groups=groups)
+    near_w, far_w = ring_gather(w_mine, swapped(w_theirs, "ctx"))
 
     core = lax.axis_index("tp")
 

time: 350 us -> 307 us (0.88)
  waiting for transfers between devices: 238 us -> 166 us
  starting transfers between devices: 28.7 us -> 73.8 us
  between operations: 13.6 us -> 0.65 us
  local copies, waits for them, and re-layouts: 8.67 us -> 19.9 us
  matrix products: 24.1 us -> 14.8 us
  other arithmetic: 11.1 us -> 6.79 us
    ppermute x0 -> x14, waiting for transfers between devices: none -> 71.1 us  [ring_gather(): held[way] = lax.ppermute(held[way], 'ctx', hops)]
    all_gather x2 -> x0, waiting for transfers between devices: 68.7 us -> none  [the longest x1 68.7 us: body(): lax.all_gather(w_mine, 'ctx', axis=0, tiled=True, axis_index_groups=groups)]
    ppermute x0 -> x14, starting transfers between devices: none -> 47.2 us  [ring_gather(): held[way] = lax.ppermute(held[way], 'ctx', hops)]
    ppermute x8, waiting for transfers between devices: 68.5 us -> 25.1 us  [swapped(): lax.ppermute(value, axis, [(i, i ^ 1) for i in range(lax.axis_size(axis))])]
    ppermute x6, waiting for transfers between devices: 100 us -> 69.9 us  [shifted(): return lax.ppermute(value, axis, pairs)]
    dynamic_update_slice x0 -> x16, local copies, waits for them, and re-layouts: none -> 11.3 us  [ring_gather(): lax.dynamic_update_slice_in_dim(full[way], held[way], origin * rows, 0)]
    ppermute x8, starting transfers between devices: 9.99 us -> 4.14 us  [swapped(): lax.ppermute(value, axis, [(i, i ^ 1) for i in range(lax.axis_size(axis))])]
    dot_general x2, matrix products: 12.4 us -> 6.82 us  [project(): jnp.dot(both_cores(near), near_w, preferred_element_type=jnp.float32)]
  transfers between devices with their start and end apart: 16 -> 28, of which waited for: 8 -> 14; matrix products, arithmetic and copies ran while one was open for 8% -> 9% of each run, Pallas kernels for 7% -> 8%
where the time goes in v2:
time: 307 us; the launch traced here: 306 us
  waiting for transfers between devices  166 us (54%)
  starting transfers between devices  73.8 us (24%)
  Pallas kernels  24.5 us (8%)
  local copies, waits for them, and re-layouts  19.9 us (6%)
  matrix products  14.8 us (5%)
  other arithmetic  6.79 us (2%)
    ppermute x14, waiting for transfers between devices, ring_gather(): held[way] = lax.ppermute(held[way], 'ctx', hops)  71.1 us
    ppermute x6, waiting for transfers between devices, shifted(): return lax.ppermute(value, axis, pairs)  69.9 us
    ppermute x14, starting transfers between devices, ring_gather(): held[way] = lax.ppermute(held[way], 'ctx', hops)  47.2 us
    ppermute x8, waiting for transfers between devices, swapped(): lax.ppermute(value, axis, [(i, i ^ 1) for i in range(lax.axis_size(axis))])  25.1 us
    pallas_call x2, Pallas kernels, attend(): pl.pallas_call(functools.partial(attend_kernel, blocks, group, tile), out...  24.5 us
    ppermute x6, starting transfers between devices, shifted(): return lax.ppermute(value, axis, pairs)  22.4 us
    dynamic_update_slice x16, local copies, waits for them, and re-layouts, ring_gather(): lax.dynamic_update_slice_in_dim(full[way], held[way], origin * rows, 0)  11.3 us
    dot_general x2, matrix products, project(): jnp.dot(both_cores(far), far_w, preferred_element_type=jnp.float32)  7.98 us
  transfers between devices with their start and end apart: 28, of which 14 were waited for; matrix products, arithmetic and copies ran while one was open for 9% of the time, Pallas kernels for 8%

profile of v2, /device:TPU:0, one launch (start us, length us, event | category | flops | bytes accessed | tf_op | source)
XLA Modules:
  0.0 306.5 jit_solution(1332654270297582567)
XLA Ops:
  0.0 0.4 broadcast.22.clone
  0.4 1.1 copy-done.13
  1.5 1.0 constant_dynamic-update-slice_fusion.15
  2.5 3.1 %collective-permute-start.15 = (bf16[256,1408]{1,0:T(8,128)(2,1)S(1)}, bf16[256,1408]{1,0:T(8,128)(2,1)}, u32[]{:S(2)}, u32[]{:S(2)}) collective-permute-start(bf16[256,1408]{1,0:T(8,128)(2,1)S(1)} %get-tuple-element.15), channel_id=1, source_target_pairs={{0,2},{2,0},{4,6},{6,4},{8,10},{10,8},{12,14},{14,12},{16,18},{18,... | collective-permute-start | bytes 2162696 | tf_op jit(solution)/shard_map/ppermute | solution.py:24
  5.6 3.5 %collective-permute-start = (bf16[512,1024]{1,0:T(8,128)(2,1)S(1)}, bf16[512,1024]{1,0:T(8,128)(2,1)S(1)}, u32[]{:S(2)}, u32[]{:S(2)}) collective-permute-start(bf16[512,1024]{1,0:T(8,128)(2,1)S(1)} %copy-done.2), channel_id=1, source_target_pairs={{0,4},{2,6},{4,8},{6,10},{8,12},{10,14},{12,16},{14,18},{16,20},{1... | collective-permute-start | bytes 3145736 | tf_op jit(solution)/shard_map/ppermute | solution.py:20
  9.1 1.6 collective-permute-start.7
  10.6 2.4 collective-permute-start.4
  13.1 2.4 collective-permute-start.5
  15.4 15.8 %collective-permute-done.4 = s32[512]{0:T(512)S(1)} collective-permute-done((s32[512]{0:T(512)S(1)}, s32[512]{0:T(512)S(1)}, u32[]{:S(2)}, u32[]{:S(2)}) %collective-permute-start.4) | collective-permute-done | bytes 2080 | tf_op jit(solution)/shard_map/ppermute | solution.py:20
  31.2 3.4 %collective-permute-start.1 = (bf16[512,1024]{1,0:T(8,128)(2,1)S(1)}, bf16[512,1024]{1,0:T(8,128)(2,1)}, u32[]{:S(2)}, u32[]{:S(2)}) collective-permute-start(bf16[512,1024]{1,0:T(8,128)(2,1)S(1)} %copy-done.2), channel_id=1, source_target_pairs={{0,2},{2,4},{4,6},{6,8},{8,10},{10,12},{12,14},{14,16},{16,18},{18... | collective-permute-start | bytes 3145736 | tf_op jit(solution)/shard_map/ppermute | solution.py:20
  34.6 4.4 %collective-permute-start.2 = (bf16[512,1024]{1,0:T(8,128)(2,1)S(1)}, bf16[512,1024]{1,0:T(8,128)(2,1)}, u32[]{:S(2)}, u32[]{:S(2)}) collective-permute-start(bf16[512,1024]{1,0:T(8,128)(2,1)S(1)} %copy-done.3), channel_id=1, source_target_pairs={{0,4},{2,6},{4,8},{6,10},{8,12},{10,14},{12,16},{14,18},{16,20},{1... | collective-permute-start | bytes 3145736 | tf_op jit(solution)/shard_map/ppermute | solution.py:20
  39.0 6.3 %collective-permute-start.3 = (bf16[512,1024]{1,0:T(8,128)(2,1)S(1)}, bf16[512,1024]{1,0:T(8,128)(2,1)}, u32[]{:S(2)}, u32[]{:S(2)}) collective-permute-start(bf16[512,1024]{1,0:T(8,128)(2,1)S(1)} %copy-done.3), channel_id=1, source_target_pairs={{0,2},{2,4},{4,6},{6,8},{8,10},{10,12},{12,14},{14,16},{16,18},{18... | collective-permute-start | bytes 3145736 | tf_op jit(solution)/shard_map/ppermute | solution.py:20
  45.4 0.1 copy.6.refs_8_
  45.7 1.0 copy-done.5
  46.6 2.0 collective-permute-start.8
  48.6 8.5 %collective-permute-done.1.refs_3_ = bf16[512,1024]{1,0:T(8,128)(2,1)} collective-permute-done((bf16[512,1024]{1,0:T(8,128)(2,1)S(1)}, bf16[512,1024]{1,0:T(8,128)(2,1)}, u32[]{:S(2)}, u32[]{:S(2)}) %collective-permute-start.1) | collective-permute-done | bytes 1048608 | tf_op jit(solution)/shard_map/ppermute | solution.py:20
  57.1 45.6 %collective-permute-done.2.refs_5_ = bf16[512,1024]{1,0:T(8,128)(2,1)} collective-permute-done((bf16[512,1024]{1,0:T(8,128)(2,1)S(1)}, bf16[512,1024]{1,0:T(8,128)(2,1)}, u32[]{:S(2)}, u32[]{:S(2)}) %collective-permute-start.2) | collective-permute-done | bytes 1048608 | tf_op jit(solution)/shard_map/ppermute | solution.py:20
  102.7 1.6 copy-done
  104.3 1.2 copy-done.6
  105.6 12.3 %shard_map.56 = bf16[512,1024]{1,0:T(8,128)(2,1)S(1)} custom-call(s32[1]{0:T(128)} %bitcast.2.refs_0_, bf16[512,2048]{1,0:T(8,128)(2,1)S(1)} %copy-done, bf16[512,1024]{1,0:T(8,128)(2,1)S(1)} %copy-done.6, bf16[512,1024]{1,0:T(8,128)(2,1)} %collective-permute-done.1.refs_3_, bf16[512,1024]{1,0:T(8,128)(2,1)S(1)} %copy-done.2, ...), custom_call_target="tpu_custom_call" | custom-call | flops 2684354560 | bytes 5242880 | tf_op jit(solution)/shard_map/pallas_call | solution.py:113
  117.9 0.3 collective-permute-done.16
  118.2 18.6 %collective-permute-start.17 = (bf16[256,1408]{1,0:T(8,128)(2,1)}, bf16[256,1408]{1,0:T(8,128)(2,1)}, u32[]{:S(2)}, u32[]{:S(2)}) collective-permute-start(bf16[256,1408]{1,0:T(8,128)(2,1)} %collective-permute-done.16), channel_id=1, source_target_pairs={{0,4},{2,6},{8,0},{10,2},{16,8},{18,10},{24,16},{26,18},{28,24},{3... | collective-permute-start | bytes 2162696 | tf_op jit(solution)/shard_map/ppermute | solution.py:44
  136.8 1.6 copy-done.1
  138.4 1.2 copy-done.4
  139.7 12.2 %shard_map.55 = bf16[512,1024]{1,0:T(8,128)(2,1)S(1)} custom-call(s32[1]{0:T(128)} %bitcast.refs_0_, bf16[512,2048]{1,0:T(8,128)(2,1)S(1)} %copy-done.1, bf16[512,1024]{1,0:T(8,128)(2,1)S(1)} %copy-done.7, bf16[512,1024]{1,0:T(8,128)(2,1)} %collective-permute-done.1.refs_3_, bf16[512,1024]{1,0:T(8,128)(2,1)S(1)} %copy-done.2, ...), custom_call_target="tpu_custom_call" | custom-call | flops 2684354560 | bytes 5242880 | tf_op jit(solution)/shard_map/pallas_call | solution.py:113
  151.9 0.1 collective-permute-start.25
  152.4 3.1 %collective-permute-start.9 = (bf16[256,1408]{1,0:T(8,128)(2,1)}, bf16[256,1408]{1,0:T(8,128)(2,1)S(1)}, u32[]{:S(2)}, u32[]{:S(2)}) collective-permute-start(bf16[256,1408]{1,0:T(8,128)(2,1)} %collective-permute-done.8), channel_id=1, source_target_pairs={{0,8},{2,10},{8,16},{10,18},{16,24},{18,26},{24,28},{26,30},{28,20... | collective-permute-start | bytes 2162696 | tf_op jit(solution)/shard_map/ppermute | solution.py:44
  155.4 0.4 broadcast.22
  155.8 1.2 constant_dynamic-update-slice_fusion.7
  157.1 2.0 constant_dynamic-update-slice_fusion.14
  159.1 1.2 constant_dynamic-update-slice_fusion.6
  160.3 0.6 collective-permute-start.24
  160.9 5.8 %collective-permute-done.9 = bf16[256,1408]{1,0:T(8,128)(2,1)S(1)} collective-permute-done((bf16[256,1408]{1,0:T(8,128)(2,1)}, bf16[256,1408]{1,0:T(8,128)(2,1)S(1)}, u32[]{:S(2)}, u32[]{:S(2)}) %collective-permute-start.9) | collective-permute-done | bytes 720928 | tf_op jit(solution)/shard_map/ppermute | solution.py:44
  166.7 2.4 collective-permute-start.10
  169.1 2.0 constant_dynamic-update-slice_fusion.13
  171.1 0.6 collective-permute-done.25
  171.7 1.2 constant_dynamic-update-slice_fusion.5
  172.9 5.3 %collective-permute-done.18 = bf16[256,1408]{1,0:T(8,128)(2,1)S(1)} collective-permute-done((bf16[256,1408]{1,0:T(8,128)(2,1)}, bf16[256,1408]{1,0:T(8,128)(2,1)S(1)}, u32[]{:S(2)}, u32[]{:S(2)}) %collective-permute-start.18) | collective-permute-done | bytes 720928 | tf_op jit(solution)/shard_map/ppermute | solution.py:44
  178.2 11.3 %collective-permute-start.19 = (bf16[256,1408]{1,0:T(8,128)(2,1)S(1)}, bf16[256,1408]{1,0:T(8,128)(2,1)S(1)}, u32[]{:S(2)}, u32[]{:S(2)}) collective-permute-start(bf16[256,1408]{1,0:T(8,128)(2,1)S(1)} %collective-permute-done.18), channel_id=1, source_target_pairs={{0,4},{2,6},{8,0},{10,2},{16,8},{18,10},{24,16},{26,18},{28,24},{3... | collective-permute-start | bytes 2162696 | tf_op jit(solution)/shard_map/ppermute | solution.py:44
  189.4 0.9 constant_dynamic-update-slice_fusion.12
  190.4 1.7 collective-permute-done.10
  192.1 1.9 collective-permute-start.11
  194.1 0.9 constant_dynamic-update-slice_fusion.11
  195.0 14.3 %collective-permute-done.19 = bf16[256,1408]{1,0:T(8,128)(2,1)S(1)} collective-permute-done((bf16[256,1408]{1,0:T(8,128)(2,1)S(1)}, bf16[256,1408]{1,0:T(8,128)(2,1)S(1)}, u32[]{:S(2)}, u32[]{:S(2)}) %collective-permute-start.19) | collective-permute-done | bytes 720928 | tf_op jit(solution)/shard_map/ppermute | solution.py:44
  209.3 1.4 broadcast_select_fusion.4
  210.7 2.1 collective-permute-start.12
  212.8 0.1 broadcast_select_fusion.2
  212.9 0.1 constant_dynamic-update-slice_fusion.3
  213.0 14.0 %collective-permute-done.20 = bf16[256,1408]{1,0:T(8,128)(2,1)S(1)} collective-permute-done((bf16[256,1408]{1,0:T(8,128)(2,1)S(1)}, bf16[256,1408]{1,0:T(8,128)(2,1)S(1)}, u32[]{:S(2)}, u32[]{:S(2)}) %collective-permute-start.20) | collective-permute-done | bytes 720928 | tf_op jit(solution)/shard_map/ppermute | solution.py:44
  227.0 0.5 collective-permute-start.21
  227.6 1.8 collective-permute-done.12
  229.4 3.7 %collective-permute-start.13 = (bf16[256,1408]{1,0:T(8,128)(2,1)S(1)}, bf16[256,1408]{1,0:T(8,128)(2,1)S(1)}, u32[]{:S(2)}, u32[]{:S(2)}) collective-permute-start(bf16[256,1408]{1,0:T(8,128)(2,1)S(1)} %collective-permute-done.12), channel_id=1, source_target_pairs={{0,8},{2,10},{8,16},{10,18},{16,24},{18,26},{24,28},{26,30},{28,20... | collective-permute-start | bytes 2162696 | tf_op jit(solution)/shard_map/ppermute | solution.py:44
  233.3 14.8 %collective-permute-done.21 = bf16[256,1408]{1,0:T(8,128)(2,1)S(1)} collective-permute-done((bf16[256,1408]{1,0:T(8,128)(2,1)S(1)}, bf16[256,1408]{1,0:T(8,128)(2,1)S(1)}, u32[]{:S(2)}, u32[]{:S(2)}) %collective-permute-start.21) | collective-permute-done | bytes 720928 | tf_op jit(solution)/shard_map/ppermute | solution.py:44
  248.3 3.4 %fusion.9 = f32[512,1408]{1,0:T(8,128)S(1)} fusion(bf16[2048,1408]{1,0:T(8,128)(2,1)S(1)} %constant_dynamic-update-slice_fusion.8, bf16[512,1024]{1,0:T(8,128)(2,1)S(1)} %get-tuple-element.10, bf16[512,1024]{1,0:T(8,128)(2,1)S(1)} %get-tuple-element.9), kind=kOutput, calls=%fused_computation.12 | convolution fusion | flops 2956984320 | bytes 10747904 | tf_op jit(solution)/shard_map/dot_general | solution.py:192
  251.7 13.2 %collective-permute-done.22 = bf16[256,1408]{1,0:T(8,128)(2,1)S(1)} collective-permute-done((bf16[256,1408]{1,0:T(8,128)(2,1)S(1)}, bf16[256,1408]{1,0:T(8,128)(2,1)S(1)}, u32[]{:S(2)}, u32[]{:S(2)}) %collective-permute-start.22) | collective-permute-done | bytes 720928 | tf_op jit(solution)/shard_map/ppermute | solution.py:44
  265.0 4.5 %fusion.1 = bf16[512,1408]{1,0:T(8,128)(2,1)} fusion(f32[512,1408]{1,0:T(8,128)S(1)} %fusion.9, bf16[2048,1408]{1,0:T(8,128)(2,1)S(1)} %constant_dynamic-update-slice_fusion, bf16[512,1024]{1,0:T(8,128)(2,1)S(1)} %get-tuple-element.8, bf16[512,1024]{1,0:T(8,128)(2,1)S(1)} %get-tuple-element.7), kind=kOutput, calls=%fused_computation.3 | convolution fusion | flops 2958426112 | bytes 12189696 | tf_op jit(solution)/shard_map/dot_general | solution.py:193
  269.5 0.3 collective-permute-start.27
  269.8 1.5 broadcast_select_fusion.8
  271.4 1.8 broadcast_select_fusion.6
  273.2 3.4 %fusion.2 = f32[512,1408]{1,0:T(8,128)S(1)} fusion(bf16[2048,1408]{1,0:T(8,128)(2,1)S(1)} %copy-done.11, bf16[512,1024]{1,0:T(8,128)(2,1)S(1)} %get-tuple-element.14, bf16[512,1024]{1,0:T(8,128)(2,1)S(1)} %get-tuple-element.13), kind=kOutput, calls=%fused_computation.5 | convolution fusion | flops 2956984320 | bytes 10747904 | tf_op jit(solution)/shard_map/dot_general | solution.py:192
  276.6 24.4 %collective-permute-done.27 = bf16[512,1408]{1,0:T(8,128)(2,1)S(1)} collective-permute-done((bf16[512,1408]{1,0:T(8,128)(2,1)}, bf16[512,1408]{1,0:T(8,128)(2,1)S(1)}, u32[]{:S(2)}, u32[]{:S(2)}) %collective-permute-start.27) | collective-permute-done | bytes 1441824 | tf_op jit(solution)/shard_map/ppermute | solution.py:24
  301.1 3.5 %broadcast_select_fusion = (bf16[512,1408]{1,0:T(8,128)(2,1)S(1)}, bf16[512,1408]{1,0:T(8,128)(2,1)S(1)}) fusion(bf16[512,1408]{1,0:T(8,128)(2,1)S(1)} %collective-permute-done.27, pred[]{:T(512)S(6)} %eq.36, f32[512,1408]{1,0:T(8,128)S(1)} %fusion.2, bf16[2048,1408]{1,0:T(8,128)(2,1)S(1)} %bitcast.8, bf16[512,1024]{1,0:T(8,128)(2,1)S(1)} %get-tuple-element.12, ...), kind=kOutput, calls=%fused_computation.19 | convolution fusion | flops 2959147008 | bytes 15073281 | tf_op jit(solution)/shard_map/dot_general | solution.py:193
  304.6 0.2 slice_select_fusion
  304.8 1.7 pad_maximum_fusion
  (62 shorter events, 0.9 us)
Async XLA Ops:
  0.0 5.6 %copy-start.2 = (bf16[512,1024]{1,0:T(8,128)(2,1)S(1)}, bf16[512,1024]{1,0:T(8,128)(2,1)}, u32[]{:S(2)}) copy-start(bf16[512,1024]{1,0:T(8,128)(2,1)} %refs_4_.3) | copy-start | bytes 3145732
  0.0 10.6 %copy-start.14 = (s32[512]{0:T(512)S(1)}, s32[512]{0:T(512)}, u32[]{:S(2)}) copy-start(s32[512]{0:T(512)} %param.8) | copy-start | bytes 6148
  0.0 34.6 %copy-start.3 = (bf16[512,1024]{1,0:T(8,128)(2,1)S(1)}, bf16[512,1024]{1,0:T(8,128)(2,1)}, u32[]{:S(2)}) copy-start(bf16[512,1024]{1,0:T(8,128)(2,1)} %refs_7_.3) | copy-start | bytes 3145732
  0.0 1.5 copy-start.13
  2.5 36.5 %copy-start.8 = (bf16[2048,1408]{1,0:T(8,128)(2,1)}, bf16[2048,1408]{1,0:T(8,128)(2,1)S(1)}, u32[]{:S(2)}) copy-start(bf16[2048,1408]{1,0:T(8,128)(2,1)S(1)} %get-tuple-element.5) | copy-start | bytes 17301508
  2.5 36.5 %collective-permute-start.15 = (bf16[256,1408]{1,0:T(8,128)(2,1)S(1)}, bf16[256,1408]{1,0:T(8,128)(2,1)}, u32[]{:S(2)}, u32[]{:S(2)}) collective-permute-start(bf16[256,1408]{1,0:T(8,128)(2,1)S(1)} %get-tuple-element.15), channel_id=1, source_target_pairs={{0,2},{2,0},{4,6},{6,4},{8,10},{10,8},{12,14},{14,12},{16,18},{18,... | collective-permute-start | bytes 2162696 | tf_op jit(solution)/shard_map/ppermute | solution.py:24
  5.6 40.1 %collective-permute-start = (bf16[512,1024]{1,0:T(8,128)(2,1)S(1)}, bf16[512,1024]{1,0:T(8,128)(2,1)S(1)}, u32[]{:S(2)}, u32[]{:S(2)}) collective-permute-start(bf16[512,1024]{1,0:T(8,128)(2,1)S(1)} %copy-done.2), channel_id=1, source_target_pairs={{0,4},{2,6},{4,8},{6,10},{8,12},{10,14},{12,16},{14,18},{16,20},{1... | collective-permute-start | bytes 3145736 | tf_op jit(solution)/shard_map/ppermute | solution.py:20
  9.1 36.5 %collective-permute-start.7 = (bf16[256,1408]{1,0:T(8,128)(2,1)}, bf16[256,1408]{1,0:T(8,128)(2,1)}, u32[]{:S(2)}, u32[]{:S(2)}) collective-permute-start(bf16[256,1408]{1,0:T(8,128)(2,1)} %get-tuple-element.6), channel_id=1, source_target_pairs={{0,8},{2,10},{8,16},{10,18},{16,24},{18,26},{24,28},{26,30},{28,20... | collective-permute-start | bytes 2162696 | tf_op jit(solution)/shard_map/ppermute | solution.py:44
  10.6 20.6 %collective-permute-start.4 = (s32[512]{0:T(512)S(1)}, s32[512]{0:T(512)S(1)}, u32[]{:S(2)}, u32[]{:S(2)}) collective-permute-start(s32[512]{0:T(512)S(1)} %copy-done.14), channel_id=1, source_target_pairs={{0,4},{2,6},{4,8},{6,10},{8,12},{10,14},{12,16},{14,18},{16,20},{1... | collective-permute-start | bytes 6152 | tf_op jit(solution)/shard_map/ppermute | solution.py:20
  13.1 21.5 %collective-permute-start.5 = (s32[512]{0:T(512)S(1)}, s32[512]{0:T(512)S(1)}, u32[]{:S(2)}, u32[]{:S(2)}) collective-permute-start(s32[512]{0:T(512)S(1)} %copy-done.14), channel_id=1, source_target_pairs={{0,2},{2,4},{4,6},{6,8},{8,10},{10,12},{12,14},{14,16},{16,18},{18... | collective-permute-start | bytes 6152 | tf_op jit(solution)/shard_map/ppermute | solution.py:20
  31.2 25.9 %collective-permute-start.1 = (bf16[512,1024]{1,0:T(8,128)(2,1)S(1)}, bf16[512,1024]{1,0:T(8,128)(2,1)}, u32[]{:S(2)}, u32[]{:S(2)}) collective-permute-start(bf16[512,1024]{1,0:T(8,128)(2,1)S(1)} %copy-done.2), channel_id=1, source_target_pairs={{0,2},{2,4},{4,6},{6,8},{8,10},{10,12},{12,14},{14,16},{16,18},{18... | collective-permute-start | bytes 3145736 | tf_op jit(solution)/shard_map/ppermute | solution.py:20
  34.6 68.1 %collective-permute-start.2 = (bf16[512,1024]{1,0:T(8,128)(2,1)S(1)}, bf16[512,1024]{1,0:T(8,128)(2,1)}, u32[]{:S(2)}, u32[]{:S(2)}) collective-permute-start(bf16[512,1024]{1,0:T(8,128)(2,1)S(1)} %copy-done.3), channel_id=1, source_target_pairs={{0,4},{2,6},{4,8},{6,10},{8,12},{10,14},{12,16},{14,18},{16,20},{1... | collective-permute-start | bytes 3145736 | tf_op jit(solution)/shard_map/ppermute | solution.py:20
  39.0 63.7 %collective-permute-start.3 = (bf16[512,1024]{1,0:T(8,128)(2,1)S(1)}, bf16[512,1024]{1,0:T(8,128)(2,1)}, u32[]{:S(2)}, u32[]{:S(2)}) collective-permute-start(bf16[512,1024]{1,0:T(8,128)(2,1)S(1)} %copy-done.3), channel_id=1, source_target_pairs={{0,2},{2,4},{4,6},{6,8},{8,10},{10,12},{12,14},{14,16},{16,18},{18... | collective-permute-start | bytes 3145736 | tf_op jit(solution)/shard_map/ppermute | solution.py:20
  45.6 72.6 %collective-permute-start.16 = (bf16[256,1408]{1,0:T(8,128)(2,1)}, bf16[256,1408]{1,0:T(8,128)(2,1)}, u32[]{:S(2)}, u32[]{:S(2)}) collective-permute-start(bf16[256,1408]{1,0:T(8,128)(2,1)} %collective-permute-done.15), channel_id=1, source_target_pairs={{0,4},{2,6},{8,0},{10,2},{16,8},{18,10},{24,16},{26,18},{28,24},{3... | collective-permute-start | bytes 2162696 | tf_op jit(solution)/shard_map/ppermute | solution.py:44
  45.7 1.0 copy-start.5
  46.6 105.7 %collective-permute-start.8 = (bf16[256,1408]{1,0:T(8,128)(2,1)}, bf16[256,1408]{1,0:T(8,128)(2,1)}, u32[]{:S(2)}, u32[]{:S(2)}) collective-permute-start(bf16[256,1408]{1,0:T(8,128)(2,1)} %collective-permute-done.7), channel_id=1, source_target_pairs={{0,8},{2,10},{8,16},{10,18},{16,24},{18,26},{24,28},{26,30},{28,20... | collective-permute-start | bytes 2162696 | tf_op jit(solution)/shard_map/ppermute | solution.py:44
  102.7 1.6 copy-start
  104.3 1.2 copy-start.6
  105.6 31.3 %copy-start.7 = (bf16[512,1024]{1,0:T(8,128)(2,1)S(1)}, bf16[512,1024]{1,0:T(8,128)(2,1)}, u32[]{:S(2)}) copy-start(bf16[512,1024]{1,0:T(8,128)(2,1)} %copy-done.5) | copy-start | bytes 3145732
  117.8 42.5 %collective-permute-start.23 = (bf16[512,1024]{1,0:T(8,128)(2,1)S(1)}, bf16[512,1024]{1,0:T(8,128)(2,1)}, u32[]{:S(2)}, u32[]{:S(2)}) collective-permute-start(bf16[512,1024]{1,0:T(8,128)(2,1)S(1)} %shard_map.56), channel_id=1, source_target_pairs={{0,2},{2,0},{4,6},{6,4},{8,10},{10,8},{12,14},{14,12},{16,18},{18,... | collective-permute-start | bytes 3145736 | tf_op jit(solution)/shard_map/ppermute | solution.py:24
  118.2 40.9 %collective-permute-start.17 = (bf16[256,1408]{1,0:T(8,128)(2,1)}, bf16[256,1408]{1,0:T(8,128)(2,1)}, u32[]{:S(2)}, u32[]{:S(2)}) collective-permute-start(bf16[256,1408]{1,0:T(8,128)(2,1)} %collective-permute-done.16), channel_id=1, source_target_pairs={{0,4},{2,6},{8,0},{10,2},{16,8},{18,10},{24,16},{26,18},{28,24},{3... | collective-permute-start | bytes 2162696 | tf_op jit(solution)/shard_map/ppermute | solution.py:44
  136.8 1.6 copy-start.1
  138.4 1.2 copy-start.4
  151.9 19.8 %collective-permute-start.25 = (bf16[512,1024]{1,0:T(8,128)(2,1)S(1)}, bf16[512,1024]{1,0:T(8,128)(2,1)S(1)}, u32[]{:S(2)}, u32[]{:S(2)}) collective-permute-start(bf16[512,1024]{1,0:T(8,128)(2,1)S(1)} %shard_map.55), channel_id=1, source_target_pairs={{0,2},{2,0},{4,6},{6,4},{8,10},{10,8},{12,14},{14,12},{16,18},{18,... | collective-permute-start | bytes 3145736 | tf_op jit(solution)/shard_map/ppermute | solution.py:24
  152.4 14.3 %collective-permute-start.9 = (bf16[256,1408]{1,0:T(8,128)(2,1)}, bf16[256,1408]{1,0:T(8,128)(2,1)S(1)}, u32[]{:S(2)}, u32[]{:S(2)}) collective-permute-start(bf16[256,1408]{1,0:T(8,128)(2,1)} %collective-permute-done.8), channel_id=1, source_target_pairs={{0,8},{2,10},{8,16},{10,18},{16,24},{18,26},{24,28},{26,30},{28,20... | collective-permute-start | bytes 2162696 | tf_op jit(solution)/shard_map/ppermute | solution.py:44
  159.1 110.7 %collective-permute-start.6 = (bf16[512,1024]{1,0:T(8,128)(2,1)S(1)}, bf16[512,1024]{1,0:T(8,128)(2,1)}, u32[]{:S(2)}, u32[]{:S(2)}) collective-permute-start(bf16[512,1024]{1,0:T(8,128)(2,1)S(1)} %shard_map.55), channel_id=1, source_target_pairs={{0,1},{1,0},{2,3},{3,2},{4,5},{5,4},{6,7},{7,6},{8,9},{9,8},{10,11... | collective-permute-start | bytes 3145736 | tf_op jit(solution)/shard_map/ppermute | solution.py:24
  159.1 19.1 %collective-permute-start.18 = (bf16[256,1408]{1,0:T(8,128)(2,1)}, bf16[256,1408]{1,0:T(8,128)(2,1)S(1)}, u32[]{:S(2)}, u32[]{:S(2)}) collective-permute-start(bf16[256,1408]{1,0:T(8,128)(2,1)} %collective-permute-done.17), channel_id=1, source_target_pairs={{0,4},{2,6},{8,0},{10,2},{16,8},{18,10},{24,16},{26,18},{28,24},{3... | collective-permute-start | bytes 2162696 | tf_op jit(solution)/shard_map/ppermute | solution.py:44
  160.3 34.7 %collective-permute-start.24 = (bf16[512,1024]{1,0:T(8,128)(2,1)}, bf16[512,1024]{1,0:T(8,128)(2,1)S(1)}, u32[]{:S(2)}, u32[]{:S(2)}) collective-permute-start(bf16[512,1024]{1,0:T(8,128)(2,1)} %collective-permute-done.23), channel_id=1, source_target_pairs={{0,1},{1,0},{2,3},{3,2},{4,5},{5,4},{6,7},{7,6},{8,9},{9,8},{10,11... | collective-permute-start | bytes 3145736 | tf_op jit(solution)/shard_map/ppermute | solution.py:24
  166.7 25.4 %collective-permute-start.10 = (bf16[256,1408]{1,0:T(8,128)(2,1)S(1)}, bf16[256,1408]{1,0:T(8,128)(2,1)S(1)}, u32[]{:S(2)}, u32[]{:S(2)}) collective-permute-start(bf16[256,1408]{1,0:T(8,128)(2,1)S(1)} %collective-permute-done.9), channel_id=1, source_target_pairs={{0,8},{2,10},{8,16},{10,18},{16,24},{18,26},{24,28},{26,30},{28,20... | collective-permute-start | bytes 2162696 | tf_op jit(solution)/shard_map/ppermute | solution.py:44
  171.7 41.1 %collective-permute-start.26 = (bf16[512,1024]{1,0:T(8,128)(2,1)S(1)}, bf16[512,1024]{1,0:T(8,128)(2,1)S(1)}, u32[]{:S(2)}, u32[]{:S(2)}) collective-permute-start(bf16[512,1024]{1,0:T(8,128)(2,1)S(1)} %collective-permute-done.25), channel_id=1, source_target_pairs={{0,1},{1,0},{2,3},{3,2},{4,5},{5,4},{6,7},{7,6},{8,9},{9,8},{10,11... | collective-permute-start | bytes 3145736 | tf_op jit(solution)/shard_map/ppermute | solution.py:24
  178.2 31.2 %collective-permute-start.19 = (bf16[256,1408]{1,0:T(8,128)(2,1)S(1)}, bf16[256,1408]{1,0:T(8,128)(2,1)S(1)}, u32[]{:S(2)}, u32[]{:S(2)}) collective-permute-start(bf16[256,1408]{1,0:T(8,128)(2,1)S(1)} %collective-permute-done.18), channel_id=1, source_target_pairs={{0,4},{2,6},{8,0},{10,2},{16,8},{18,10},{24,16},{26,18},{28,24},{3... | collective-permute-start | bytes 2162696 | tf_op jit(solution)/shard_map/ppermute | solution.py:44
  192.1 18.6 %collective-permute-start.11 = (bf16[256,1408]{1,0:T(8,128)(2,1)S(1)}, bf16[256,1408]{1,0:T(8,128)(2,1)S(1)}, u32[]{:S(2)}, u32[]{:S(2)}) collective-permute-start(bf16[256,1408]{1,0:T(8,128)(2,1)S(1)} %collective-permute-done.10), channel_id=1, source_target_pairs={{0,8},{2,10},{8,16},{10,18},{16,24},{18,26},{24,28},{26,30},{28,20... | collective-permute-start | bytes 2162696 | tf_op jit(solution)/shard_map/ppermute | solution.py:44
  195.0 32.5 %copy-start.9 = (bf16[2048,1408]{1,0:T(8,128)(2,1)S(1)}, bf16[2048,1408]{1,0:T(8,128)(2,1)}, u32[]{:S(2)}) copy-start(bf16[2048,1408]{1,0:T(8,128)(2,1)} %constant_dynamic-update-slice_fusion.11) | copy-start | bytes 17301508
  195.0 76.3 %collective-permute-start.14 = (bf16[512,1024]{1,0:T(8,128)(2,1)S(1)}, bf16[512,1024]{1,0:T(8,128)(2,1)}, u32[]{:S(2)}, u32[]{:S(2)}) collective-permute-start(bf16[512,1024]{1,0:T(8,128)(2,1)S(1)} %shard_map.56), channel_id=1, source_target_pairs={{0,1},{1,0},{2,3},{3,2},{4,5},{5,4},{6,7},{7,6},{8,9},{9,8},{10,11... | collective-permute-start | bytes 3145736 | tf_op jit(solution)/shard_map/ppermute | solution.py:24
  209.3 17.7 %collective-permute-start.20 = (bf16[256,1408]{1,0:T(8,128)(2,1)S(1)}, bf16[256,1408]{1,0:T(8,128)(2,1)S(1)}, u32[]{:S(2)}, u32[]{:S(2)}) collective-permute-start(bf16[256,1408]{1,0:T(8,128)(2,1)S(1)} %collective-permute-done.19), channel_id=1, source_target_pairs={{0,4},{2,6},{8,0},{10,2},{16,8},{18,10},{24,16},{26,18},{28,24},{3... | collective-permute-start | bytes 2162696 | tf_op jit(solution)/shard_map/ppermute | solution.py:44
  210.7 18.7 %collective-permute-start.12 = (bf16[256,1408]{1,0:T(8,128)(2,1)S(1)}, bf16[256,1408]{1,0:T(8,128)(2,1)S(1)}, u32[]{:S(2)}, u32[]{:S(2)}) collective-permute-start(bf16[256,1408]{1,0:T(8,128)(2,1)S(1)} %collective-permute-done.11), channel_id=1, source_target_pairs={{0,8},{2,10},{8,16},{10,18},{16,24},{18,26},{24,28},{26,30},{28,20... | collective-permute-start | bytes 2162696 | tf_op jit(solution)/shard_map/ppermute | solution.py:44
  227.0 21.1 %collective-permute-start.21 = (bf16[256,1408]{1,0:T(8,128)(2,1)S(1)}, bf16[256,1408]{1,0:T(8,128)(2,1)S(1)}, u32[]{:S(2)}, u32[]{:S(2)}) collective-permute-start(bf16[256,1408]{1,0:T(8,128)(2,1)S(1)} %collective-permute-done.20), channel_id=1, source_target_pairs={{0,4},{2,6},{8,0},{10,2},{16,8},{18,10},{24,16},{26,18},{28,24},{3... | collective-permute-start | bytes 2162696 | tf_op jit(solution)/shard_map/ppermute | solution.py:44
  229.4 18.8 %collective-permute-start.13 = (bf16[256,1408]{1,0:T(8,128)(2,1)S(1)}, bf16[256,1408]{1,0:T(8,128)(2,1)S(1)}, u32[]{:S(2)}, u32[]{:S(2)}) collective-permute-start(bf16[256,1408]{1,0:T(8,128)(2,1)S(1)} %collective-permute-done.12), channel_id=1, source_target_pairs={{0,8},{2,10},{8,16},{10,18},{16,24},{18,26},{24,28},{26,30},{28,20... | collective-permute-start | bytes 2162696 | tf_op jit(solution)/shard_map/ppermute | solution.py:44
  248.1 16.8 %collective-permute-start.22 = (bf16[256,1408]{1,0:T(8,128)(2,1)S(1)}, bf16[256,1408]{1,0:T(8,128)(2,1)S(1)}, u32[]{:S(2)}, u32[]{:S(2)}) collective-permute-start(bf16[256,1408]{1,0:T(8,128)(2,1)S(1)} %collective-permute-done.21), channel_id=1, source_target_pairs={{0,4},{2,6},{8,0},{10,2},{16,8},{18,10},{24,16},{26,18},{28,24},{3... | collective-permute-start | bytes 2162696 | tf_op jit(solution)/shard_map/ppermute | solution.py:44
  248.3 16.7 %copy-start.10 = (bf16[2048,1408]{1,0:T(8,128)(2,1)}, bf16[2048,1408]{1,0:T(8,128)(2,1)S(1)}, u32[]{:S(2)}) copy-start(bf16[2048,1408]{1,0:T(8,128)(2,1)S(1)} %constant_dynamic-update-slice_fusion.8) | copy-start | bytes 17301508
  265.0 4.5 %copy-start.12 = (bf16[2048,1408]{1,0:T(8,128)(2,1)}, bf16[2048,1408]{1,0:T(8,128)(2,1)S(1)}, u32[]{:S(2)}) copy-start(bf16[2048,1408]{1,0:T(8,128)(2,1)S(1)} %constant_dynamic-update-slice_fusion) | copy-start | bytes 17301508
  269.5 31.6 %collective-permute-start.27 = (bf16[512,1408]{1,0:T(8,128)(2,1)}, bf16[512,1408]{1,0:T(8,128)(2,1)S(1)}, u32[]{:S(2)}, u32[]{:S(2)}) collective-permute-start(bf16[512,1408]{1,0:T(8,128)(2,1)} %fusion.1), channel_id=1, source_target_pairs={{0,2},{2,0},{4,6},{6,4},{8,10},{10,8},{12,14},{14,12},{16,18},{18,... | collective-permute-start | bytes 4325384 | tf_op jit(solution)/shard_map/ppermute | solution.py:24
  269.8 3.4 %copy-start.11 = (bf16[2048,1408]{1,0:T(8,128)(2,1)S(1)}, bf16[2048,1408]{1,0:T(8,128)(2,1)}, u32[]{:S(2)}) copy-start(bf16[2048,1408]{1,0:T(8,128)(2,1)} %copy-done.10) | copy-start | bytes 17301508
  271.3 29.7 %slice-start = ((s8[5767168]{0:T(1024)(128)(4,1)}), s8[4194304]{0:T(1024)(128)(4,1)S(1)}, s32[]{:S(2)}) async-start(s8[5767168]{0:T(1024)(128)(4,1)} %bitcast.7), calls=%async_computation | async-start | bytes 8388608
  273.2 27.9 %slice-start.1 = ((s8[5767168]{0:T(1024)(128)(4,1)}), s8[1572864]{0:T(1024)(128)(4,1)S(1)}, s32[]{:S(2)}) async-start(s8[5767168]{0:T(1024)(128)(4,1)} %bitcast.7), calls=%async_computation.1 | async-start | bytes 3145728

commit v3 on v2

--- a/solution.py
+++ b/solution.py
@@ -32,6 +32,7 @@
     at = jnp.where(place % 2 == 0, place // 2, n - 1 - place // 2)
     rows, width = forward.shape
     held = [forward, backward]
+    trail = []
     full = [jnp.zeros((n * rows, width), forward.dtype) for _ in held]
     for step in range(n):
         for way, sign in enumerate((1, -1)):
@@ -45,14 +46,16 @@
             k = (at - sign * step + n) % n
             origin = jnp.where(k < n // 2, 2 * k, 2 * (n - 1 - k) + 1)
             full[way] = lax.dynamic_update_slice_in_dim(full[way], held[way], origin * rows, 0)
-    return full
-
-
-def attend_kernel(blocks, group, tile, *refs):
+        trail.append(list(held))
+    return full, trail
+
+
+def attend_kernel(blocks, group, tile, waits, *refs):
     q_ref = refs[1]
     k_refs = refs[2 : 2 + blocks]
     v_refs = refs[2 + blocks : 2 + 2 * blocks]
-    qdoc_ref, kdoc_ref, o_ref, bias = refs[2 + 2 * blocks :]
+    qdoc_ref, kdoc_ref = refs[2 + 2 * blocks : 4 + 2 * blocks]
+    o_ref, bias = refs[4 + 2 * blocks + waits :]
     rows = q_ref.shape[0]
     span = LOOKBACK_SPAN + tile
 
@@ -93,7 +96,7 @@
             o_ref[near : near + tile, lanes] = (numer / total).astype(o_ref.dtype)
 
 
-def attend(first, stride, query_states, keys, values, query_docs, key_docs):
+def attend(first, stride, query_states, keys, values, query_docs, key_docs, after=()):
     rows, width = query_states.shape
     kv_here = keys[0].shape[1] // HEAD_SIZE
     group = width // HEAD_SIZE // kv_here
@@ -111,14 +114,15 @@
 
     kv_spec = pl.BlockSpec((rows, HEAD_SIZE), head)
     return pl.pallas_call(
-        functools.partial(attend_kernel, blocks, group, tile),
+        functools.partial(attend_kernel, blocks, group, tile, len(after)),
         out_shape=jax.ShapeDtypeStruct((rows, heads * wide), jnp.bfloat16),
         grid_spec=pltpu.PrefetchScalarGridSpec(
             num_scalar_prefetch=1,
             grid=(heads,),
             in_specs=[pl.BlockSpec((rows, wide), head)]
             + [kv_spec] * (2 * blocks)
-            + [pl.BlockSpec((rows, 1), whole), pl.BlockSpec((1, blocks * rows), whole)],
+            + [pl.BlockSpec((rows, 1), whole), pl.BlockSpec((1, blocks * rows), whole)]
+            + [pl.BlockSpec(memory_space=pl.ANY)] * len(after),
             out_specs=pl.BlockSpec((rows, wide), lambda i, first_ref: (0, i)),
             scratch_shapes=[pltpu.VMEM((rows // tile, tile, span), jnp.float32)],
         ),
@@ -128,7 +132,7 @@
             bytes_accessed=2 * heads * rows * (2 * wide + 2 * blocks * HEAD_SIZE),
             transcendentals=heads * group * rows * span,
         ),
-    )(first, query_states, *keys, *values, query_docs, key_docs)
+    )(first, query_states, *keys, *values, query_docs, key_docs, *after)
 
 
 def body(query_states, rotated_key_states, value_state_rows, doc_ids, w_out):
@@ -168,7 +172,7 @@
     shift = columns - half
     w_mine = lax.dynamic_slice_in_dim(w_out, parity * shift, half, 1)
     w_theirs = lax.dynamic_slice_in_dim(w_out, (1 - parity) * shift, half, 1)
-    near_w, far_w = ring_gather(w_mine, swapped(w_theirs, "ctx"))
+    (near_w, far_w), trail = ring_gather(w_mine, swapped(w_theirs, "ctx"))
 
     core = lax.axis_index("tp")
 
@@ -178,14 +182,13 @@
         high = jnp.where(core == 0, other, part)
         return jnp.concatenate([low, high], 1)
 
-    def heads_of(which):
-        return attend(
-            which.reshape(1).astype(jnp.int32), 2, query_states, keys, values, query_docs, key_docs
-        )
-
-    mine_near = heads_of(parity)
+    def heads_of(which, after):
+        first = which.reshape(1).astype(jnp.int32)
+        return attend(first, 2, query_states, keys, values, query_docs, key_docs, after)
+
+    mine_near = heads_of(parity, trail[min(3, len(trail) - 1)])
     theirs_far = swapped(mine_near, "ctx")
-    mine_far = heads_of(1 - parity)
+    mine_far = heads_of(1 - parity, trail[min(4, len(trail) - 1)])
     theirs_near = swapped(mine_far, "ctx")
 
     def project(near, far):

time: 307 us -> 299 us (0.974)
  starting transfers between devices: 73.8 us -> 56.4 us
  waiting for transfers between devices: 166 us -> 180 us
  local copies, waits for them, and re-layouts: 19.9 us -> 10.7 us
    ppermute x14, waiting for transfers between devices: 71.1 us -> 98 us  [ring_gather(): held[way] = lax.ppermute(held[way], 'ctx', hops)]
    ppermute x6, waiting for transfers between devices: 69.9 us -> 53.9 us  [shifted(): return lax.ppermute(value, axis, pairs)]
    ppermute x14, starting transfers between devices: 47.2 us -> 31.8 us  [ring_gather(): held[way] = lax.ppermute(held[way], 'ctx', hops)]
    unnamed x34 -> x28, local copies, waits for them, and re-layouts: 7.72 us -> 0.98 us
    ppermute x6, starting transfers between devices: 22.4 us -> 18.8 us  [shifted(): return lax.ppermute(value, axis, pairs)]
    ppermute x8, waiting for transfers between devices: 25.1 us -> 28.4 us  [swapped(): lax.ppermute(value, axis, [(i, i ^ 1) for i in range(lax.axis_size(axis))])]
  transfers between devices with their start and end apart: 28 -> 28, of which waited for: 14 -> 12; matrix products, arithmetic and copies ran while one was open for 9% -> 9% of each run, Pallas kernels for 8% -> 9%
where the time goes in v3:
time: 299 us; the launch traced here: 298 us
  waiting for transfers between devices  180 us (60%)
  starting transfers between devices  56.4 us (19%)
  Pallas kernels  25.9 us (9%)
  matrix products  17.3 us (6%)
  local copies, waits for them, and re-layouts  10.7 us (4%)
  other arithmetic  6.88 us (2%)
    ppermute x14, waiting for transfers between devices, ring_gather(): held[way] = lax.ppermute(held[way], 'ctx', hops)  98 us
    ppermute x6, waiting for transfers between devices, shifted(): return lax.ppermute(value, axis, pairs)  53.9 us
    ppermute x14, starting transfers between devices, ring_gather(): held[way] = lax.ppermute(held[way], 'ctx', hops)  31.8 us
    ppermute x8, waiting for transfers between devices, swapped(): lax.ppermute(value, axis, [(i, i ^ 1) for i in range(lax.axis_size(axis))])  28.4 us
    pallas_call x2, Pallas kernels, attend(): pl.pallas_call(functools.partial(attend_kernel, blocks, group, tile, len(...  25.9 us
    ppermute x6, starting transfers between devices, shifted(): return lax.ppermute(value, axis, pairs)  18.8 us
    dot_general x2, matrix products, project(): jnp.dot(both_cores(near), near_w, preferred_element_type=jnp.float32)  9.3 us
    dynamic_update_slice x16, local copies, waits for them, and re-layouts, ring_gather(): lax.dynamic_update_slice_in_dim(full[way], held[way], origin * rows, 0)  8.76 us
  transfers between devices with their start and end apart: 28, of which 12 were waited for; matrix products, arithmetic and copies ran while one was open for 9% of the time, Pallas kernels for 9%

profile of v3, /device:TPU:0, one launch (start us, length us, event | category | flops | bytes accessed | tf_op | source)
XLA Modules:
  0.0 298.4 jit_solution(2036896992270014540)
XLA Ops:
  0.0 0.4 broadcast.22.clone
  0.4 0.9 copy-done.7
  1.3 0.2 constant_dynamic-update-slice_fusion.15
  1.6 3.1 %collective-permute-start.9 = (bf16[256,1408]{1,0:T(8,128)(2,1)S(1)}, bf16[256,1408]{1,0:T(8,128)(2,1)S(1)}, u32[]{:S(2)}, u32[]{:S(2)}) collective-permute-start(bf16[256,1408]{1,0:T(8,128)(2,1)S(1)} %get-tuple-element.15), channel_id=1, source_target_pairs={{0,2},{2,0},{4,6},{6,4},{8,10},{10,8},{12,14},{14,12},{16,18},{18,... | collective-permute-start | bytes 2162696 | tf_op jit(solution)/shard_map/ppermute | solution.py:24
  4.6 1.6 collective-permute-start.6
  6.2 14.6 %collective-permute-done.9 = bf16[256,1408]{1,0:T(8,128)(2,1)S(1)} collective-permute-done((bf16[256,1408]{1,0:T(8,128)(2,1)S(1)}, bf16[256,1408]{1,0:T(8,128)(2,1)S(1)}, u32[]{:S(2)}, u32[]{:S(2)}) %collective-permute-start.9) | collective-permute-done | bytes 720928 | tf_op jit(solution)/shard_map/ppermute | solution.py:24
  20.8 1.7 collective-permute-start.10
  22.5 4.4 %collective-permute-start.1 = (bf16[512,1024]{1,0:T(8,128)(2,1)S(1)}, bf16[512,1024]{1,0:T(8,128)(2,1)}, u32[]{:S(2)}, u32[]{:S(2)}) collective-permute-start(bf16[512,1024]{1,0:T(8,128)(2,1)S(1)} %copy-done.1), channel_id=1, source_target_pairs={{0,2},{2,4},{4,6},{6,8},{8,10},{10,12},{12,14},{14,16},{16,18},{18... | collective-permute-start | bytes 3145736 | tf_op jit(solution)/shard_map/ppermute | solution.py:20
  26.9 32.6 %collective-permute-done.10 = bf16[256,1408]{1,0:T(8,128)(2,1)} collective-permute-done((bf16[256,1408]{1,0:T(8,128)(2,1)S(1)}, bf16[256,1408]{1,0:T(8,128)(2,1)}, u32[]{:S(2)}, u32[]{:S(2)}) %collective-permute-start.10) | collective-permute-done | bytes 720928 | tf_op jit(solution)/shard_map/ppermute | solution.py:45
  59.6 2.6 collective-permute-start.11
  62.2 1.9 collective-permute-start.4
  64.1 1.3 collective-permute-start.5
  65.8 0.1 copy.6.refs_8_
  66.0 10.2 %collective-permute-done.4 = s32[512]{0:T(512)S(1)} collective-permute-done((s32[512]{0:T(512)S(1)}, s32[512]{0:T(512)S(1)}, u32[]{:S(2)}, u32[]{:S(2)}) %collective-permute-start.4) | collective-permute-done | bytes 2080 | tf_op jit(solution)/shard_map/ppermute | solution.py:20
  76.2 4.4 %collective-permute-start = (bf16[512,1024]{1,0:T(8,128)(2,1)S(1)}, bf16[512,1024]{1,0:T(8,128)(2,1)S(1)}, u32[]{:S(2)}, u32[]{:S(2)}) collective-permute-start(bf16[512,1024]{1,0:T(8,128)(2,1)S(1)} %copy-done.1), channel_id=1, source_target_pairs={{0,4},{2,6},{4,8},{6,10},{8,12},{10,14},{12,16},{14,18},{16,20},{1... | collective-permute-start | bytes 3145736 | tf_op jit(solution)/shard_map/ppermute | solution.py:20
  80.7 1.5 collective-permute-start.3
  82.3 5.1 %collective-permute-start.2 = (bf16[512,1024]{1,0:T(8,128)(2,1)}, bf16[512,1024]{1,0:T(8,128)(2,1)S(1)}, u32[]{:S(2)}, u32[]{:S(2)}) collective-permute-start(bf16[512,1024]{1,0:T(8,128)(2,1)} %refs_7_.3), channel_id=1, source_target_pairs={{0,4},{2,6},{4,8},{6,10},{8,12},{10,14},{12,16},{14,18},{16,20},{1... | collective-permute-start | bytes 3145736 | tf_op jit(solution)/shard_map/ppermute | solution.py:20
  87.5 1.6 collective-permute-start.8
  89.0 0.5 collective-permute-start.12
  89.6 0.4 broadcast.22
  90.0 0.1 constant_dynamic-update-slice_fusion.7
  90.1 2.0 constant_dynamic-update-slice_fusion.14
  92.1 2.0 constant_dynamic-update-slice_fusion.13
  94.1 9.9 %collective-permute-done.8.refs_10_ = bf16[256,1408]{1,0:T(8,128)(2,1)S(1)} collective-permute-done((bf16[256,1408]{1,0:T(8,128)(2,1)}, bf16[256,1408]{1,0:T(8,128)(2,1)S(1)}, u32[]{:S(2)}, u32[]{:S(2)}) %collective-permute-start.8) | collective-permute-done | bytes 720928 | tf_op jit(solution)/shard_map/ppermute | solution.py:45
  104.0 1.5 collective-permute-start.14
  105.6 21.1 %collective-permute-done.refs_2_ = bf16[512,1024]{1,0:T(8,128)(2,1)S(1)} collective-permute-done((bf16[512,1024]{1,0:T(8,128)(2,1)S(1)}, bf16[512,1024]{1,0:T(8,128)(2,1)S(1)}, u32[]{:S(2)}, u32[]{:S(2)}) %collective-permute-start) | collective-permute-done | bytes 1048608 | tf_op jit(solution)/shard_map/ppermute | solution.py:20
  126.7 22.6 %collective-permute-done.2.refs_5_ = bf16[512,1024]{1,0:T(8,128)(2,1)S(1)} collective-permute-done((bf16[512,1024]{1,0:T(8,128)(2,1)}, bf16[512,1024]{1,0:T(8,128)(2,1)S(1)}, u32[]{:S(2)}, u32[]{:S(2)}) %collective-permute-start.2) | collective-permute-done | bytes 1048608 | tf_op jit(solution)/shard_map/ppermute | solution.py:20
  149.3 11.7 %collective-permute-done.12.refs_11_ = bf16[256,1408]{1,0:T(8,128)(2,1)S(1)} collective-permute-done((bf16[256,1408]{1,0:T(8,128)(2,1)}, bf16[256,1408]{1,0:T(8,128)(2,1)S(1)}, u32[]{:S(2)}, u32[]{:S(2)}) %collective-permute-start.12) | collective-permute-done | bytes 720928 | tf_op jit(solution)/shard_map/ppermute | solution.py:45
  160.9 13.0 %shard_map.55 = bf16[512,1024]{1,0:T(8,128)(2,1)} custom-call(s32[1]{0:T(128)} %bitcast.refs_0_, bf16[512,2048]{1,0:T(8,128)(2,1)S(1)} %copy-done, bf16[512,1024]{1,0:T(8,128)(2,1)S(1)} %collective-permute-done.refs_2_, bf16[512,1024]{1,0:T(8,128)(2,1)} %collective-permute-done.1.refs_3_, bf16[512,1024]{1,0:T(8,128)(2,1)S(1)} %copy-done.1, ...), custom_call_target="tpu_custom_call" | custom-call | flops 2684354560 | bytes 5242880 | tf_op jit(solution)/shard_map/pallas_call | solution.py:116
  174.0 15.6 %collective-permute-start.18 = (bf16[256,1408]{1,0:T(8,128)(2,1)S(1)}, bf16[256,1408]{1,0:T(8,128)(2,1)S(1)}, u32[]{:S(2)}, u32[]{:S(2)}) collective-permute-start(bf16[256,1408]{1,0:T(8,128)(2,1)S(1)} %collective-permute-done.12.refs_11_), channel_id=1, source_target_pairs={{0,4},{2,6},{8,0},{10,2},{16,8},{18,10},{24,16},{26,18},{28,24},{3... | collective-permute-start | bytes 2162696 | tf_op jit(solution)/shard_map/ppermute | solution.py:45
  189.6 1.2 constant_dynamic-update-slice_fusion.6
  190.8 0.1 constant_dynamic-update-slice_fusion.12
  191.0 1.2 constant_dynamic-update-slice_fusion.5
  192.3 9.5 %collective-permute-done.18.refs_11_ = bf16[256,1408]{1,0:T(8,128)(2,1)S(1)} collective-permute-done((bf16[256,1408]{1,0:T(8,128)(2,1)S(1)}, bf16[256,1408]{1,0:T(8,128)(2,1)S(1)}, u32[]{:S(2)}, u32[]{:S(2)}) %collective-permute-start.18) | collective-permute-done | bytes 720928 | tf_op jit(solution)/shard_map/ppermute | solution.py:45
  201.8 12.8 %shard_map.56 = bf16[512,1024]{1,0:T(8,128)(2,1)} custom-call(s32[1]{0:T(128)} %bitcast.2.refs_0_, bf16[512,2048]{1,0:T(8,128)(2,1)S(1)} %copy-done, bf16[512,1024]{1,0:T(8,128)(2,1)S(1)} %collective-permute-done.refs_2_, bf16[512,1024]{1,0:T(8,128)(2,1)} %collective-permute-done.1.refs_3_, bf16[512,1024]{1,0:T(8,128)(2,1)S(1)} %copy-done.1, ...), custom_call_target="tpu_custom_call" | custom-call | flops 2684354560 | bytes 5242880 | tf_op jit(solution)/shard_map/pallas_call | solution.py:116
  214.6 0.3 collective-permute-start.23
  214.9 0.1 constant_dynamic-update-slice_fusion.11
  215.0 2.5 collective-permute-start.20
  217.6 0.1 constant_dynamic-update-slice_fusion.4
  217.7 1.2 constant_dynamic-update-slice_fusion.10
  218.9 0.1 constant_dynamic-update-slice_fusion.3
  219.0 15.4 %collective-permute-done.16 = bf16[256,1408]{1,0:T(8,128)(2,1)S(1)} collective-permute-done((bf16[256,1408]{1,0:T(8,128)(2,1)}, bf16[256,1408]{1,0:T(8,128)(2,1)S(1)}, u32[]{:S(2)}, u32[]{:S(2)}) %collective-permute-start.16) | collective-permute-done | bytes 720928 | tf_op jit(solution)/shard_map/ppermute | solution.py:45
  234.4 2.0 collective-permute-start.21
  236.5 0.1 constant_dynamic-update-slice_fusion.9
  236.6 0.1 constant_dynamic-update-slice_fusion.2
  236.7 0.6 collective-permute-start.19
  237.3 0.3 broadcast_select_fusion.2
  237.6 13.4 %collective-permute-done.21 = bf16[256,1408]{1,0:T(8,128)(2,1)S(1)} collective-permute-done((bf16[256,1408]{1,0:T(8,128)(2,1)S(1)}, bf16[256,1408]{1,0:T(8,128)(2,1)S(1)}, u32[]{:S(2)}, u32[]{:S(2)}) %collective-permute-start.21) | collective-permute-done | bytes 720928 | tf_op jit(solution)/shard_map/ppermute | solution.py:45
  250.9 2.0 collective-permute-start.22
  253.0 0.1 constant_dynamic-update-slice_fusion.1
  253.1 0.1 constant_dynamic-update-slice_fusion.8
  253.2 0.1 broadcast_select_fusion.4
  253.3 3.4 %fusion.9 = f32[512,1408]{1,0:T(8,128)S(1)} fusion(bf16[2048,1408]{1,0:T(8,128)(2,1)S(1)} %constant_dynamic-update-slice_fusion.8, bf16[512,1024]{1,0:T(8,128)(2,1)S(1)} %get-tuple-element.10, bf16[512,1024]{1,0:T(8,128)(2,1)S(1)} %get-tuple-element.9), kind=kOutput, calls=%fused_computation.12 | convolution fusion | flops 2956984320 | bytes 10747904 | tf_op jit(solution)/shard_map/dot_general | solution.py:195
  256.8 5.5 %collective-permute-done.22 = bf16[256,1408]{1,0:T(8,128)(2,1)S(1)} collective-permute-done((bf16[256,1408]{1,0:T(8,128)(2,1)S(1)}, bf16[256,1408]{1,0:T(8,128)(2,1)S(1)}, u32[]{:S(2)}, u32[]{:S(2)}) %collective-permute-start.22) | collective-permute-done | bytes 720928 | tf_op jit(solution)/shard_map/ppermute | solution.py:45
  262.2 0.1 constant_dynamic-update-slice_fusion
  262.3 4.5 %fusion.1 = bf16[512,1408]{1,0:T(8,128)(2,1)} fusion(f32[512,1408]{1,0:T(8,128)S(1)} %fusion.9, bf16[2048,1408]{1,0:T(8,128)(2,1)S(1)} %constant_dynamic-update-slice_fusion, bf16[512,1024]{1,0:T(8,128)(2,1)S(1)} %get-tuple-element.8, bf16[512,1024]{1,0:T(8,128)(2,1)S(1)} %get-tuple-element.7), kind=kOutput, calls=%fused_computation.3 | convolution fusion | flops 2958426112 | bytes 12189696 | tf_op jit(solution)/shard_map/dot_general | solution.py:196
  266.8 1.7 collective-permute-start.27
  268.6 1.7 broadcast_select_fusion.8
  270.3 1.5 broadcast_select_fusion.6
  271.8 5.9 %fusion.2 = f32[512,1408]{1,0:T(8,128)S(1)} fusion(bf16[2048,1408]{1,0:T(8,128)(2,1)} %copy-done.5, bf16[512,1024]{1,0:T(8,128)(2,1)S(1)} %get-tuple-element.14, bf16[512,1024]{1,0:T(8,128)(2,1)S(1)} %get-tuple-element.13), kind=kOutput, calls=%fused_computation.5 | convolution fusion | flops 2956984320 | bytes 10747904 | tf_op jit(solution)/shard_map/dot_general | solution.py:195
  277.7 13.9 %collective-permute-done.27 = bf16[512,1408]{1,0:T(8,128)(2,1)S(1)} collective-permute-done((bf16[512,1408]{1,0:T(8,128)(2,1)}, bf16[512,1408]{1,0:T(8,128)(2,1)S(1)}, u32[]{:S(2)}, u32[]{:S(2)}) %collective-permute-start.27) | collective-permute-done | bytes 1441824 | tf_op jit(solution)/shard_map/ppermute | solution.py:24
  291.6 3.5 %broadcast_select_fusion = (bf16[512,1408]{1,0:T(8,128)(2,1)S(1)}, bf16[512,1408]{1,0:T(8,128)(2,1)S(1)}) fusion(bf16[512,1408]{1,0:T(8,128)(2,1)S(1)} %collective-permute-done.27, pred[]{:T(512)S(6)} %eq.36, f32[512,1408]{1,0:T(8,128)S(1)} %fusion.2, bf16[2048,1408]{1,0:T(8,128)(2,1)S(1)} %bitcast.8, bf16[512,1024]{1,0:T(8,128)(2,1)S(1)} %get-tuple-element.12, ...), kind=kOutput, calls=%fused_computation.19 | convolution fusion | flops 2959147008 | bytes 15073281 | tf_op jit(solution)/shard_map/dot_general | solution.py:196
  295.1 1.5 slice_select_fusion
  296.6 1.7 pad_maximum_fusion
  (56 shorter events, 0.4 us)
Async XLA Ops:
  0.0 1.3 copy-start.7
  0.0 22.5 %copy-start.1 = (bf16[512,1024]{1,0:T(8,128)(2,1)S(1)}, bf16[512,1024]{1,0:T(8,128)(2,1)}, u32[]{:S(2)}) copy-start(bf16[512,1024]{1,0:T(8,128)(2,1)} %refs_4_.3) | copy-start | bytes 3145732
  0.0 62.1 %copy-start.11 = (s32[512]{0:T(512)S(1)}, s32[512]{0:T(512)}, u32[]{:S(2)}) copy-start(s32[512]{0:T(512)} %param.8) | copy-start | bytes 6148
  1.5 19.2 %copy-start.3 = (bf16[2048,1408]{1,0:T(8,128)(2,1)}, bf16[2048,1408]{1,0:T(8,128)(2,1)S(1)}, u32[]{:S(2)}) copy-start(bf16[2048,1408]{1,0:T(8,128)(2,1)S(1)} %get-tuple-element.5) | copy-start | bytes 17301508
  1.6 19.2 %collective-permute-start.9 = (bf16[256,1408]{1,0:T(8,128)(2,1)S(1)}, bf16[256,1408]{1,0:T(8,128)(2,1)S(1)}, u32[]{:S(2)}, u32[]{:S(2)}) collective-permute-start(bf16[256,1408]{1,0:T(8,128)(2,1)S(1)} %get-tuple-element.15), channel_id=1, source_target_pairs={{0,2},{2,0},{4,6},{6,4},{8,10},{10,8},{12,14},{14,12},{16,18},{18,... | collective-permute-start | bytes 2162696 | tf_op jit(solution)/shard_map/ppermute | solution.py:24
  4.6 22.3 %collective-permute-start.6 = (bf16[256,1408]{1,0:T(8,128)(2,1)S(1)}, bf16[256,1408]{1,0:T(8,128)(2,1)}, u32[]{:S(2)}, u32[]{:S(2)}) collective-permute-start(bf16[256,1408]{1,0:T(8,128)(2,1)S(1)} %get-tuple-element.6), channel_id=1, source_target_pairs={{0,8},{2,10},{8,16},{10,18},{16,24},{18,26},{24,28},{26,30},{28,20... | collective-permute-start | bytes 2162696 | tf_op jit(solution)/shard_map/ppermute | solution.py:45
  20.8 44.6 %copy-start.9 = (bf16[256,1408]{1,0:T(8,128)(2,1)}, bf16[256,1408]{1,0:T(8,128)(2,1)S(1)}, u32[]{:S(2)}) copy-start(bf16[256,1408]{1,0:T(8,128)(2,1)S(1)} %collective-permute-done.9) | copy-start | bytes 2162692
  20.8 38.8 %collective-permute-start.10 = (bf16[256,1408]{1,0:T(8,128)(2,1)S(1)}, bf16[256,1408]{1,0:T(8,128)(2,1)}, u32[]{:S(2)}, u32[]{:S(2)}) collective-permute-start(bf16[256,1408]{1,0:T(8,128)(2,1)S(1)} %collective-permute-done.9), channel_id=1, source_target_pairs={{0,4},{2,6},{8,0},{10,2},{16,8},{18,10},{24,16},{26,18},{28,24},{3... | collective-permute-start | bytes 2162696 | tf_op jit(solution)/shard_map/ppermute | solution.py:45
  22.5 59.8 %collective-permute-start.1 = (bf16[512,1024]{1,0:T(8,128)(2,1)S(1)}, bf16[512,1024]{1,0:T(8,128)(2,1)}, u32[]{:S(2)}, u32[]{:S(2)}) collective-permute-start(bf16[512,1024]{1,0:T(8,128)(2,1)S(1)} %copy-done.1), channel_id=1, source_target_pairs={{0,2},{2,4},{4,6},{6,8},{8,10},{10,12},{12,14},{14,16},{16,18},{18... | collective-permute-start | bytes 3145736 | tf_op jit(solution)/shard_map/ppermute | solution.py:20
  26.9 60.5 %collective-permute-start.7 = (bf16[256,1408]{1,0:T(8,128)(2,1)}, bf16[256,1408]{1,0:T(8,128)(2,1)}, u32[]{:S(2)}, u32[]{:S(2)}) collective-permute-start(bf16[256,1408]{1,0:T(8,128)(2,1)} %collective-permute-done.6), channel_id=1, source_target_pairs={{0,8},{2,10},{8,16},{10,18},{16,24},{18,26},{24,28},{26,30},{28,20... | collective-permute-start | bytes 2162696 | tf_op jit(solution)/shard_map/ppermute | solution.py:45
  59.6 29.5 %collective-permute-start.11 = (bf16[256,1408]{1,0:T(8,128)(2,1)}, bf16[256,1408]{1,0:T(8,128)(2,1)}, u32[]{:S(2)}, u32[]{:S(2)}) collective-permute-start(bf16[256,1408]{1,0:T(8,128)(2,1)} %collective-permute-done.10), channel_id=1, source_target_pairs={{0,4},{2,6},{8,0},{10,2},{16,8},{18,10},{24,16},{26,18},{28,24},{3... | collective-permute-start | bytes 2162696 | tf_op jit(solution)/shard_map/ppermute | solution.py:45
  62.2 14.1 %collective-permute-start.4 = (s32[512]{0:T(512)S(1)}, s32[512]{0:T(512)S(1)}, u32[]{:S(2)}, u32[]{:S(2)}) collective-permute-start(s32[512]{0:T(512)S(1)} %copy-done.11), channel_id=1, source_target_pairs={{0,4},{2,6},{4,8},{6,10},{8,12},{10,14},{12,16},{14,18},{16,20},{1... | collective-permute-start | bytes 6152 | tf_op jit(solution)/shard_map/ppermute | solution.py:20
  64.1 16.6 %collective-permute-start.5 = (s32[512]{0:T(512)S(1)}, s32[512]{0:T(512)S(1)}, u32[]{:S(2)}, u32[]{:S(2)}) collective-permute-start(s32[512]{0:T(512)S(1)} %copy-done.11), channel_id=1, source_target_pairs={{0,2},{2,4},{4,6},{6,8},{8,10},{10,12},{12,14},{14,16},{16,18},{18... | collective-permute-start | bytes 6152 | tf_op jit(solution)/shard_map/ppermute | solution.py:20
  65.4 95.5 %copy-start = (bf16[512,2048]{1,0:T(8,128)(2,1)S(1)}, bf16[512,2048]{1,0:T(8,128)(2,1)}, u32[]{:S(2)}) copy-start(bf16[512,2048]{1,0:T(8,128)(2,1)} %refs_1_.3) | copy-start | bytes 6291460
  66.0 24.0 %copy-start.10 = (bf16[256,1408]{1,0:T(8,128)(2,1)S(1)}, bf16[256,1408]{1,0:T(8,128)(2,1)}, u32[]{:S(2)}) copy-start(bf16[256,1408]{1,0:T(8,128)(2,1)} %copy-done.9) | copy-start | bytes 2162692
  66.0 94.9 %copy-start.2 = (bf16[512,1024]{1,0:T(8,128)(2,1)S(1)}, bf16[512,1024]{1,0:T(8,128)(2,1)}, u32[]{:S(2)}) copy-start(bf16[512,1024]{1,0:T(8,128)(2,1)} %refs_7_.3) | copy-start | bytes 3145732
  76.2 50.4 %collective-permute-start = (bf16[512,1024]{1,0:T(8,128)(2,1)S(1)}, bf16[512,1024]{1,0:T(8,128)(2,1)S(1)}, u32[]{:S(2)}, u32[]{:S(2)}) collective-permute-start(bf16[512,1024]{1,0:T(8,128)(2,1)S(1)} %copy-done.1), channel_id=1, source_target_pairs={{0,4},{2,6},{4,8},{6,10},{8,12},{10,14},{12,16},{14,18},{16,20},{1... | collective-permute-start | bytes 3145736 | tf_op jit(solution)/shard_map/ppermute | solution.py:20
  80.7 46.0 %collective-permute-start.3 = (bf16[512,1024]{1,0:T(8,128)(2,1)}, bf16[512,1024]{1,0:T(8,128)(2,1)S(1)}, u32[]{:S(2)}, u32[]{:S(2)}) collective-permute-start(bf16[512,1024]{1,0:T(8,128)(2,1)} %refs_7_.3), channel_id=1, source_target_pairs={{0,2},{2,4},{4,6},{6,8},{8,10},{10,12},{12,14},{14,16},{16,18},{18... | collective-permute-start | bytes 3145736 | tf_op jit(solution)/shard_map/ppermute | solution.py:20
  82.3 67.0 %collective-permute-start.2 = (bf16[512,1024]{1,0:T(8,128)(2,1)}, bf16[512,1024]{1,0:T(8,128)(2,1)S(1)}, u32[]{:S(2)}, u32[]{:S(2)}) collective-permute-start(bf16[512,1024]{1,0:T(8,128)(2,1)} %refs_7_.3), channel_id=1, source_target_pairs={{0,4},{2,6},{4,8},{6,10},{8,12},{10,14},{12,16},{14,18},{16,20},{1... | collective-permute-start | bytes 3145736 | tf_op jit(solution)/shard_map/ppermute | solution.py:20
  87.5 16.6 %collective-permute-start.8 = (bf16[256,1408]{1,0:T(8,128)(2,1)}, bf16[256,1408]{1,0:T(8,128)(2,1)S(1)}, u32[]{:S(2)}, u32[]{:S(2)}) collective-permute-start(bf16[256,1408]{1,0:T(8,128)(2,1)} %collective-permute-done.7), channel_id=1, source_target_pairs={{0,8},{2,10},{8,16},{10,18},{16,24},{18,26},{24,28},{26,30},{28,20... | collective-permute-start | bytes 2162696 | tf_op jit(solution)/shard_map/ppermute | solution.py:45
  89.0 71.9 %collective-permute-start.12 = (bf16[256,1408]{1,0:T(8,128)(2,1)}, bf16[256,1408]{1,0:T(8,128)(2,1)S(1)}, u32[]{:S(2)}, u32[]{:S(2)}) collective-permute-start(bf16[256,1408]{1,0:T(8,128)(2,1)} %collective-permute-done.11), channel_id=1, source_target_pairs={{0,4},{2,6},{8,0},{10,2},{16,8},{18,10},{24,16},{26,18},{28,24},{3... | collective-permute-start | bytes 2162696 | tf_op jit(solution)/shard_map/ppermute | solution.py:45
  104.0 86.9 %collective-permute-start.14 = (bf16[256,1408]{1,0:T(8,128)(2,1)S(1)}, bf16[256,1408]{1,0:T(8,128)(2,1)S(1)}, u32[]{:S(2)}, u32[]{:S(2)}) collective-permute-start(bf16[256,1408]{1,0:T(8,128)(2,1)S(1)} %collective-permute-done.8.refs_10_), channel_id=1, source_target_pairs={{0,8},{2,10},{8,16},{10,18},{16,24},{18,26},{24,28},{26,30},{28,20... | collective-permute-start | bytes 2162696 | tf_op jit(solution)/shard_map/ppermute | solution.py:45
  160.9 29.9 %copy-start.4 = (bf16[2048,1408]{1,0:T(8,128)(2,1)S(1)}, bf16[2048,1408]{1,0:T(8,128)(2,1)}, u32[]{:S(2)}) copy-start(bf16[2048,1408]{1,0:T(8,128)(2,1)} %constant_dynamic-update-slice_fusion.13) | copy-start | bytes 17301508
  174.0 43.6 %collective-permute-start.25 = (bf16[512,1024]{1,0:T(8,128)(2,1)}, bf16[512,1024]{1,0:T(8,128)(2,1)S(1)}, u32[]{:S(2)}, u32[]{:S(2)}) collective-permute-start(bf16[512,1024]{1,0:T(8,128)(2,1)} %shard_map.55), channel_id=1, source_target_pairs={{0,2},{2,0},{4,6},{6,4},{8,10},{10,8},{12,14},{14,12},{16,18},{18,... | collective-permute-start | bytes 3145736 | tf_op jit(solution)/shard_map/ppermute | solution.py:24
  174.0 27.8 %collective-permute-start.18 = (bf16[256,1408]{1,0:T(8,128)(2,1)S(1)}, bf16[256,1408]{1,0:T(8,128)(2,1)S(1)}, u32[]{:S(2)}, u32[]{:S(2)}) collective-permute-start(bf16[256,1408]{1,0:T(8,128)(2,1)S(1)} %collective-permute-done.12.refs_11_), channel_id=1, source_target_pairs={{0,4},{2,6},{8,0},{10,2},{16,8},{18,10},{24,16},{26,18},{28,24},{3... | collective-permute-start | bytes 2162696 | tf_op jit(solution)/shard_map/ppermute | solution.py:45
  191.0 26.6 %collective-permute-start.15 = (bf16[256,1408]{1,0:T(8,128)(2,1)S(1)}, bf16[256,1408]{1,0:T(8,128)(2,1)}, u32[]{:S(2)}, u32[]{:S(2)}) collective-permute-start(bf16[256,1408]{1,0:T(8,128)(2,1)S(1)} %collective-permute-done.14.refs_10_), channel_id=1, source_target_pairs={{0,8},{2,10},{8,16},{10,18},{16,24},{18,26},{24,28},{26,30},{28,20... | collective-permute-start | bytes 2162696 | tf_op jit(solution)/shard_map/ppermute | solution.py:45
  192.2 76.4 %collective-permute-start.13 = (bf16[512,1024]{1,0:T(8,128)(2,1)}, bf16[512,1024]{1,0:T(8,128)(2,1)}, u32[]{:S(2)}, u32[]{:S(2)}) collective-permute-start(bf16[512,1024]{1,0:T(8,128)(2,1)} %shard_map.55), channel_id=1, source_target_pairs={{0,1},{1,0},{2,3},{3,2},{4,5},{5,4},{6,7},{7,6},{8,9},{9,8},{10,11... | collective-permute-start | bytes 3145736 | tf_op jit(solution)/shard_map/ppermute | solution.py:24
  214.6 21.9 %collective-permute-start.23 = (bf16[512,1024]{1,0:T(8,128)(2,1)}, bf16[512,1024]{1,0:T(8,128)(2,1)S(1)}, u32[]{:S(2)}, u32[]{:S(2)}) collective-permute-start(bf16[512,1024]{1,0:T(8,128)(2,1)} %shard_map.56), channel_id=1, source_target_pairs={{0,2},{2,0},{4,6},{6,4},{8,10},{10,8},{12,14},{14,12},{16,18},{18,... | collective-permute-start | bytes 3145736 | tf_op jit(solution)/shard_map/ppermute | solution.py:24
  215.0 19.4 %collective-permute-start.20 = (bf16[256,1408]{1,0:T(8,128)(2,1)S(1)}, bf16[256,1408]{1,0:T(8,128)(2,1)S(1)}, u32[]{:S(2)}, u32[]{:S(2)}) collective-permute-start(bf16[256,1408]{1,0:T(8,128)(2,1)S(1)} %collective-permute-done.18.refs_11_), channel_id=1, source_target_pairs={{0,4},{2,6},{8,0},{10,2},{16,8},{18,10},{24,16},{26,18},{28,24},{3... | collective-permute-start | bytes 2162696 | tf_op jit(solution)/shard_map/ppermute | solution.py:45
  217.5 16.9 %collective-permute-start.16 = (bf16[256,1408]{1,0:T(8,128)(2,1)}, bf16[256,1408]{1,0:T(8,128)(2,1)S(1)}, u32[]{:S(2)}, u32[]{:S(2)}) collective-permute-start(bf16[256,1408]{1,0:T(8,128)(2,1)} %collective-permute-done.15), channel_id=1, source_target_pairs={{0,8},{2,10},{8,16},{10,18},{16,24},{18,26},{24,28},{26,30},{28,20... | collective-permute-start | bytes 2162696 | tf_op jit(solution)/shard_map/ppermute | solution.py:45
  217.6 19.2 %collective-permute-start.26 = (bf16[512,1024]{1,0:T(8,128)(2,1)S(1)}, bf16[512,1024]{1,0:T(8,128)(2,1)S(1)}, u32[]{:S(2)}, u32[]{:S(2)}) collective-permute-start(bf16[512,1024]{1,0:T(8,128)(2,1)S(1)} %collective-permute-done.25), channel_id=1, source_target_pairs={{0,1},{1,0},{2,3},{3,2},{4,5},{5,4},{6,7},{7,6},{8,9},{9,8},{10,11... | collective-permute-start | bytes 3145736 | tf_op jit(solution)/shard_map/ppermute | solution.py:24
  234.4 18.6 %collective-permute-start.17 = (bf16[256,1408]{1,0:T(8,128)(2,1)S(1)}, bf16[256,1408]{1,0:T(8,128)(2,1)S(1)}, u32[]{:S(2)}, u32[]{:S(2)}) collective-permute-start(bf16[256,1408]{1,0:T(8,128)(2,1)S(1)} %collective-permute-done.16), channel_id=1, source_target_pairs={{0,8},{2,10},{8,16},{10,18},{16,24},{18,26},{24,28},{26,30},{28,20... | collective-permute-start | bytes 2162696 | tf_op jit(solution)/shard_map/ppermute | solution.py:45
  234.4 16.5 %collective-permute-start.21 = (bf16[256,1408]{1,0:T(8,128)(2,1)S(1)}, bf16[256,1408]{1,0:T(8,128)(2,1)S(1)}, u32[]{:S(2)}, u32[]{:S(2)}) collective-permute-start(bf16[256,1408]{1,0:T(8,128)(2,1)S(1)} %collective-permute-done.20), channel_id=1, source_target_pairs={{0,4},{2,6},{8,0},{10,2},{16,8},{18,10},{24,16},{26,18},{28,24},{3... | collective-permute-start | bytes 2162696 | tf_op jit(solution)/shard_map/ppermute | solution.py:45
  236.6 16.6 %collective-permute-start.24 = (bf16[512,1024]{1,0:T(8,128)(2,1)S(1)}, bf16[512,1024]{1,0:T(8,128)(2,1)S(1)}, u32[]{:S(2)}, u32[]{:S(2)}) collective-permute-start(bf16[512,1024]{1,0:T(8,128)(2,1)S(1)} %collective-permute-done.23), channel_id=1, source_target_pairs={{0,1},{1,0},{2,3},{3,2},{4,5},{5,4},{6,7},{7,6},{8,9},{9,8},{10,11... | collective-permute-start | bytes 3145736 | tf_op jit(solution)/shard_map/ppermute | solution.py:24
  236.7 33.5 %collective-permute-start.19 = (bf16[512,1024]{1,0:T(8,128)(2,1)}, bf16[512,1024]{1,0:T(8,128)(2,1)S(1)}, u32[]{:S(2)}, u32[]{:S(2)}) collective-permute-start(bf16[512,1024]{1,0:T(8,128)(2,1)} %shard_map.56), channel_id=1, source_target_pairs={{0,1},{1,0},{2,3},{3,2},{4,5},{5,4},{6,7},{7,6},{8,9},{9,8},{10,11... | collective-permute-start | bytes 3145736 | tf_op jit(solution)/shard_map/ppermute | solution.py:24
  250.9 11.3 %collective-permute-start.22 = (bf16[256,1408]{1,0:T(8,128)(2,1)S(1)}, bf16[256,1408]{1,0:T(8,128)(2,1)S(1)}, u32[]{:S(2)}, u32[]{:S(2)}) collective-permute-start(bf16[256,1408]{1,0:T(8,128)(2,1)S(1)} %collective-permute-done.21), channel_id=1, source_target_pairs={{0,4},{2,6},{8,0},{10,2},{16,8},{18,10},{24,16},{26,18},{28,24},{3... | collective-permute-start | bytes 2162696 | tf_op jit(solution)/shard_map/ppermute | solution.py:45
  253.2 3.6 %copy-start.5 = (bf16[2048,1408]{1,0:T(8,128)(2,1)}, bf16[2048,1408]{1,0:T(8,128)(2,1)S(1)}, u32[]{:S(2)}) copy-start(bf16[2048,1408]{1,0:T(8,128)(2,1)S(1)} %constant_dynamic-update-slice_fusion.8) | copy-start | bytes 17301508
  262.3 4.5 %copy-start.6 = (bf16[2048,1408]{1,0:T(8,128)(2,1)}, bf16[2048,1408]{1,0:T(8,128)(2,1)S(1)}, u32[]{:S(2)}) copy-start(bf16[2048,1408]{1,0:T(8,128)(2,1)S(1)} %constant_dynamic-update-slice_fusion) | copy-start | bytes 17301508
  266.8 24.7 %collective-permute-start.27 = (bf16[512,1408]{1,0:T(8,128)(2,1)}, bf16[512,1408]{1,0:T(8,128)(2,1)S(1)}, u32[]{:S(2)}, u32[]{:S(2)}) collective-permute-start(bf16[512,1408]{1,0:T(8,128)(2,1)} %fusion.1), channel_id=1, source_target_pairs={{0,2},{2,0},{4,6},{6,4},{8,10},{10,8},{12,14},{14,12},{16,18},{18,... | collective-permute-start | bytes 4325384 | tf_op jit(solution)/shard_map/ppermute | solution.py:24
  270.3 21.3 %slice-start = ((s8[5767168]{0:T(1024)(128)(4,1)}), s8[4194304]{0:T(1024)(128)(4,1)S(1)}, s32[]{:S(2)}) async-start(s8[5767168]{0:T(1024)(128)(4,1)} %bitcast.7), calls=%async_computation | async-start | bytes 8388608
  271.8 19.8 %slice-start.1 = ((s8[5767168]{0:T(1024)(128)(4,1)}), s8[1572864]{0:T(1024)(128)(4,1)S(1)}, s32[]{:S(2)}) async-start(s8[5767168]{0:T(1024)(128)(4,1)} %bitcast.7), calls=%async_computation.1 | async-start | bytes 3145728
  291.6 3.5 %copy-start.8 = (bf16[512,1408]{1,0:T(8,128)(2,1)}, bf16[512,1408]{1,0:T(8,128)(2,1)S(1)}, u32[]{:S(2)}) copy-start(bf16[512,1408]{1,0:T(8,128)(2,1)S(1)} %collective-permute-done.27) | copy-start | bytes 4325380
